TPU v7x, 1024 devices: a whole 4x8x16 slice. The times are simulated.
1024 devices in a mesh: wide: 32 (over z, core), group: 32 (over x, y).
Axes of the slice: x: 4, y: 8, z: 16, core: 2. Of those that a mesh axis runs over, the one named last changes fastest.
Arguments:
- patches: bfloat16 [16384, 16, 1152], P(('wide', 'group')), may hold values from -6 to 6
- counts: int32 [16384], P(('wide', 'group')), may hold values from 4 to 16, as said below
- key_weight: bfloat16 [1152, 1152], replicated, may hold values from -0.1875 to 0.1875
- value_weight: bfloat16 [1152, 1152], replicated, may hold values from -0.1875 to 0.1875
- probe_query: bfloat16 [16, 72], replicated, may hold values from -5 to 5
- text_embed: bfloat16 [16384, 1152], P(('wide', 'group')), may hold values from -6 to 6
- labels: int32 [16384], P(('wide', 'group')), may hold values from 0 to 511
- logit_scale: float32 [], replicated, may hold values from 4 to 16
- logit_bias: float32 [], replicated, may hold values from -6 to -2
Outputs:
- row_loss: float32 [16384], P(('wide', 'group'))
- text_grad: float32 [16384, 1152], P(('wide', 'group'))
Inputs may be any that keep to these rules, and one draw needn't show every extreme that they name: `counts`: counts come in blocks of 16 images. Among the 32 blocks b with the same b // 32, exactly 8 hold only images of 16 patches; every other block's images have 4 or 6 patches, 16 * (5) patches in all.
All inputs are finite; a program needn't handle non-finite values.
Results may differ from a plain program's by a relative error of at most 0.0085.
Values may be sent and summed in bfloat16 or wider, within the bound.
No kernel may reach another device: no remote copies, remote signals or barrier semaphores. Data moves between devices by JAX's collectives and lax.ppermute only.
A program may use at most 32 MiB of HBM per device.

v0:
```python
import jax
import jax.numpy as jnp
from jax import lax
from jax.sharding import PartitionSpec as P


def pool_rows(patch_rows, patch_counts, key_weight, value_weight, probe_query):
    lead_dims = patch_rows.shape[:-2]
    patch_count = patch_rows.shape[-2]
    model_width = patch_rows.shape[-1]
    head_count = probe_query.shape[0]
    head_size = probe_query.shape[1]
    flat_rows = patch_rows.reshape(-1, model_width)
    key_rows = jnp.dot(flat_rows, key_weight, preferred_element_type=jnp.float32).astype(
        jnp.bfloat16
    )
    value_rows = jnp.dot(flat_rows, value_weight, preferred_element_type=jnp.float32).astype(
        jnp.bfloat16
    )
    key_rows = key_rows.reshape(-1, patch_count, head_count, head_size)
    value_rows = value_rows.reshape(-1, patch_count, head_count, head_size)
    scores = jnp.einsum("rphe,he->rhp", key_rows, probe_query, preferred_element_type=jnp.float32)
    scores = scores * (1.0 / head_size**0.5)
    is_valid = lax.broadcasted_iota(jnp.int32, (1, 1, patch_count), 2) < patch_counts.reshape(
        -1, 1, 1
    )
    scores = jnp.where(is_valid, scores, -1e30)
    attend = jax.nn.softmax(scores, axis=-1).astype(jnp.bfloat16)
    pooled = jnp.einsum("rhp,rphe->rhe", attend, value_rows, preferred_element_type=jnp.float32)
    return pooled.reshape(lead_dims + (model_width,)).astype(jnp.bfloat16)


def unit_rows(embed):
    embed32 = embed.astype(jnp.float32)
    length = jnp.sqrt(jnp.sum(embed32 * embed32, axis=-1, keepdims=True) + 1e-06)
    return (embed32 / length, length)


def row_dot(left, right):
    return lax.dot_general(
        left, right, (((1,), (1,)), ((), ())), preferred_element_type=jnp.float32
    )


def shards(
    patches,
    counts,
    key_weight,
    value_weight,
    probe_query,
    text_embed,
    labels,
    logit_scale,
    logit_bias,
):
    pooled = pool_rows(patches, counts, key_weight, value_weight, probe_query)
    image_dir, image_length = unit_rows(pooled)
    image_unit = image_dir.astype(jnp.bfloat16)
    unit, text_length = unit_rows(text_embed)
    text_unit = unit.astype(jnp.bfloat16)
    raw = row_dot(image_unit, lax.all_gather(text_unit, "wide", axis=0, tiled=True))
    logits = logit_scale * raw + logit_bias
    batch_size = raw.shape[1]
    column = lax.broadcasted_iota(jnp.int32, (1, batch_size), 1)
    signs = jnp.where(column == labels[:, None], 1.0, -1.0).astype(jnp.float32)
    row_loss = jnp.sum(jax.nn.softplus(-signs * logits), axis=-1)
    image32 = image_unit.astype(jnp.float32)
    slope = -signs * jax.nn.sigmoid(-signs * logits)
    unit_grad = lax.psum_scatter(
        logit_scale * jnp.dot(slope.T, image32, precision=lax.Precision.HIGHEST),
        "wide",
        scatter_dimension=0,
        tiled=True,
    )
    along = jnp.sum(unit_grad * unit, axis=-1, keepdims=True)
    text_grad = (unit_grad - along * unit) / text_length
    return (row_loss, text_grad)


def solution(mesh):
    return jax.shard_map(
        shards,
        mesh=mesh,
        in_specs=(
            P(("wide", "group"), None, None),
            P(("wide", "group")),
            P(),
            P(),
            P(),
            P(("wide", "group"), None),
            P(("wide", "group")),
            P(),
            P(),
        ),
        out_specs=(P(("wide", "group")), P(("wide", "group"), None)),
        check_vma=False,
    )
```

profile of v0, /device:TPU:1, one launch (start us, length us, event | category | flops | bytes accessed | tf_op | source)
XLA Modules:
  0.0 218.0 jit_solution(2911373464960216376)
XLA Ops:
  7.2 0.0 copy-start
  7.2 0.0 all-gather.2.cloned.1.call-start
  7.2 1.0 fusion.15
  8.3 1.5 fusion.33
  9.7 0.0 all-gather.2.cloned.1.call-update
  9.8 0.0 reduce-scatter.2.cloned.1.call-start
  9.8 0.0 copy-done
  9.8 2.1 convolution_convert_fusion.1
  11.9 2.8 %reshape.56 = bf16[16,16,16,72]{3,2,1,0:T(8,128)(2,1)} reshape(bf16[256,1152]{1,0:T(8,128)(2,1)S(1)} %convolution_convert_fusion.1) | data formatting | bytes 1179648 | tf_op jit(solution)/shard_map/reshape | solution.py:20
  14.7 3.0 %convolution_convert_fusion = bf16[256,1152]{1,0:T(8,128)(2,1)S(1)} fusion(bf16[256,1152]{1,0:T(8,128)(2,1)} %bitcast.21, bf16[1152,1152]{1,0:T(8,128)(2,1)} %param.12), kind=kOutput, calls=%fused_computation.3 | convolution fusion | flops 679772160 | bytes 3833856 | tf_op jit(solution)/shard_map/dot_general | solution.py:17
  17.7 2.9 %reshape.57 = bf16[16,16,16,72]{3,2,1,0:T(8,128)(2,1)} reshape(bf16[256,1152]{1,0:T(8,128)(2,1)S(1)} %convolution_convert_fusion) | data formatting | bytes 1179648 | tf_op jit(solution)/shard_map/reshape | solution.py:21
  20.5 0.1 iota_compare_fusion.2
  20.6 3.8 %fusion.11 = f32[16,1,16,16]{3,1,2,0:T(1,128)S(1)} fusion(bf16[16,16,16,72]{3,2,1,0:T(8,128)(2,1)} %reshape.56, bf16[16,72,1,1]{1,0,2,3:T(8,128)(2,1)S(1)} %bitcast.22), kind=kOutput, calls=%fused_computation.15 | convolution fusion | flops 589824 | bytes 608512 | tf_op jit(solution)/shard_map/rphe,he->rhp/dot_general | solution.py:22
  24.4 0.2 fusion.6
  24.6 1.6 fusion.9
  26.3 0.2 multiply_reduce_fusion
  26.5 0.1 reshape.58
  27.9 67.3 %all-gather.2.cloned.1.call-done = bf16[512,1152]{1,0:T(8,128)(2,1)} async-done(((bf16[16,1152]{1,0:T(8,128)(2,1)}), bf16[512,1152]{1,0:T(8,128)(2,1)}) %all-gather.2.cloned.1.call-update) | async-done | bytes 1179664 | tf_op jit(solution)/shard_map/all_gather | solution.py:61
  95.2 2.3 %fusion.19 = (f32[16]{0:T(128)}, f32[16,512]{1,0:T(8,128)S(1)}) fusion(f32[]{:T(128)S(6)} %copy.26, bf16[512,1152]{1,0:T(8,128)(2,1)} %all-gather.2.cloned.1.call-done, f32[16,1152]{1,0:T(8,128)S(1)} %reshape.58, f32[16]{0:T(128)S(1)} %add_sqrt_fusion.1, f32[]{:T(128)S(6)} %copy.25, s32[16]{0:T(128)S(1)} %copy-done.2), kind=kOutput, calls=%fused_computation.33 | convolution fusion | flops 19017712 | bytes 1286344 | tf_op jit(solution)/shard_map/dot_general | solution.py:40
  97.5 2.6 %convolution_multiply_fusion = f32[512,1152]{1,0:T(8,128)} fusion(f32[]{:T(128)S(6)} %copy.25, f32[16,512]{1,0:T(8,128)S(1)} %get-tuple-element.5, s32[16]{0:T(128)S(1)} %copy-done.2, f32[16,1152]{1,0:T(8,128)S(1)} %reshape.58, f32[16]{0:T(128)S(1)} %add_sqrt_fusion.1), kind=kOutput, calls=%fused_computation.2 | convolution fusion | flops 113930240 | bytes 2465924 | tf_op jit(solution)/shard_map/dot_general | solution.py:70
  100.1 0.0 reduce-scatter.2.cloned.1.call-update
  100.1 108.3 %reduce-scatter.2.cloned.1.call-done = f32[16,1152]{1,0:T(8,128)} async-done(((f32[512,1152]{1,0:T(8,128)}), f32[16,1152]{1,0:T(8,128)}) %reduce-scatter.2.cloned.1.call-update) | async-done | bytes 73744 | tf_op jit(solution)/shard_map/reduce_scatter | solution.py:69
  208.5 1.1 multiply_reduce_fusion.1
  209.5 1.6 subtract_divide_fusion
  (10 shorter events, 0.0 us)
Async XLA Ops:
  7.2 2.7 %copy-start = (bf16[1152,1152]{1,0:T(8,128)(2,1)S(1)}, bf16[1152,1152]{1,0:T(8,128)(2,1)}, u32[]{:S(2)}) copy-start(bf16[1152,1152]{1,0:T(8,128)(2,1)} %param.11) | copy-start | bytes 7962628
  7.2 88.0 %all-gather.2.cloned.1.call-start = ((), (), s32[]{:S(2)}) async-start(), calls=%async_computation.1 | async-start | bytes 1216512 | tf_op jit(solution)/shard_map/all_gather | solution.py:61
  9.8 198.7 %reduce-scatter.2.cloned.1.call-start = ((), (), s32[]{:S(2)}) async-start(), calls=%async_computation.2 | async-start | bytes 2433024 | tf_op jit(solution)/shard_map/reduce_scatter | solution.py:69
  14.7 5.8 %copy-start.3 = (s32[16]{0:T(128)S(1)}, s32[16]{0:T(128)}, u32[]{:S(2)}) copy-start(s32[16]{0:T(128)} %param.10) | copy-start | bytes 196
  14.7 5.9 %copy-start.4 = (bf16[16,72]{1,0:T(8,128)(2,1)S(1)}, bf16[16,72]{1,0:T(8,128)(2,1)}, u32[]{:S(2)}) copy-start(bf16[16,72]{1,0:T(8,128)(2,1)} %param.13) | copy-start | bytes 6916
  20.5 74.6 %copy-start.2 = (s32[16]{0:T(128)S(1)}, s32[16]{0:T(128)}, u32[]{:S(2)}) copy-start(s32[16]{0:T(128)} %param.15) | copy-start | bytes 196
  97.5 111.0 %copy-start.1 = (bf16[16,1152]{1,0:T(8,128)(2,1)S(1)}, bf16[16,1152]{1,0:T(8,128)(2,1)}, u32[]{:S(2)}) copy-start(bf16[16,1152]{1,0:T(8,128)(2,1)} %param.14) | copy-start | bytes 110596
Sparse Core Ops, SparseCore 0:
  11.3 83.8 all-gather.1
  100.3 108.1 reduce-scatter.1
where the time goes:
time: 220 us; the launch traced here: 218 us
  waiting for transfers between devices  176 us (80%)
  matrix products  15.4 us (7%)
  between operations  15.4 us (7%)
  local copies, waits for them, and re-layouts  5.81 us (3%)
  other arithmetic  5.7 us (3%)
    reduce_scatter x1, waiting for transfers between devices, shards(): lax.psum_scatter(logit_scale * jnp.dot(slope.T, image32, precision=lax.Pr...  108 us
    all_gather x1, waiting for transfers between devices, shards(): lax.all_gather(text_unit, 'wide', axis=0, tiled=True)  67.3 us
  transfers between devices with their start and end apart: 2, of which 2 were waited for; matrix products, arithmetic and copies ran while one was open for 8% of the time, Pallas kernels for 0%

commit v1 on v0

v1 whole, which is shorter than its diff:
```python
import functools

import jax
import jax.numpy as jnp
from jax import lax
from jax.experimental import pallas as pl
from jax.experimental.pallas import tpu as pltpu
from jax.sharding import PartitionSpec as P

LANES = 128
NEAR = 4
CHUNKS = 3

VMEM = pl.BlockSpec(memory_space=pltpu.VMEM)
SMEM = pl.BlockSpec(memory_space=pltpu.SMEM)
ANY = pl.BlockSpec(memory_space=pl.ANY)


def dot(left, right):
    return jnp.dot(left, right, preferred_element_type=jnp.float32)


def row_dot(left, right):
    return lax.dot_general(
        left, right, (((1,), (1,)), ((), ())), preferred_element_type=jnp.float32
    )


def iota(shape, dim):
    return lax.broadcasted_iota(jnp.int32, shape, dim)


def pool_kernel(
    text_hbm, query_hbm, patches_hbm, key_hbm, value_hbm, counts_ref, labels_ref,
    out_ref, text_ref, query_ref, patches_ref, key_ref, value_ref, sems,
):
    images, patch_count, width = patches_ref.shape
    heads, head_size = query_ref.shape
    rows = images * patch_count
    block = width // CHUNKS
    copies = []

    def fetch(source, target):
        copies.append(pltpu.make_async_copy(source, target, sems.at[len(copies)]))
        copies[-1].start()

    fetch(patches_hbm, patches_ref)
    for source, target in ((key_hbm, key_ref), (value_hbm, value_ref)):
        for c in range(CHUNKS):
            at = pl.ds(c * block, block)
            fetch(source.at[:, at], target.at[:, at])
            if len(copies) == 2:
                fetch(text_hbm, text_ref)
                fetch(query_hbm, query_ref)
    patches_copy, text_copy, query_copy = copies[0], copies[2], copies[3]
    copies = copies[1:2] + copies[4:]

    text_copy.wait()
    text = text_ref[...].astype(jnp.float32)
    length = jnp.sqrt(jnp.sum(text * text, axis=-1, keepdims=True) + 1e-06)
    out_ref[0:images, 0:width] = (text / length).astype(jnp.bfloat16)
    wide = lax.axis_index("wide")
    lane = iota((images, LANES), 1)
    row = iota((images, LANES), 0)
    place = (lane == wide) | (lane == row + 32)
    out_ref[0:images, width:] = jnp.where(place, 1.0, 0.0).astype(jnp.bfloat16)
    first = jnp.zeros((images, LANES), jnp.int32)
    second = jnp.zeros((images, LANES), jnp.int32)
    valid = jnp.zeros((images, patch_count, heads), jnp.int32)
    image = iota((images, patch_count, heads), 0)
    for i in range(images):
        label = labels_ref[i]
        high = lax.shift_right_logical(label, 4)
        first = jnp.where(row == i, high, first)
        second = jnp.where(row == i, label - 16 * high + 32, second)
        valid = jnp.where(image == i, counts_ref[i], valid)
    place = (lane == first) | (lane == second)
    out_ref[images:, width:] = jnp.where(place, 1.0, 0.0).astype(jnp.bfloat16)

    column = iota((1, width), 1)
    head_of = jnp.zeros((1, width), jnp.int32)
    for h in range(1, heads):
        head_of += (column >= h * head_size).astype(jnp.int32)
    inner = column - head_of * head_size
    query_copy.wait()
    spread = jnp.where(iota((head_size, width), 0) == inner, 1.0, 0.0).astype(jnp.bfloat16)
    own = iota((heads, width), 0) == head_of
    query = jnp.where(own, dot(query_ref[...], spread), 0.0).astype(jnp.bfloat16)
    own = jnp.where(own, 1.0, 0.0).astype(jnp.bfloat16)

    patches_copy.wait()
    flat = patches_ref[...].reshape(rows, width)
    scores = jnp.zeros((rows, heads), jnp.float32)
    for c in range(CHUNKS):
        copies[c].wait()
        at = slice(c * block, (c + 1) * block)
        keys = dot(flat, key_ref[:, at]).astype(jnp.bfloat16)
        scores += row_dot(keys, query[:, at])
    scores = (scores * (1.0 / head_size**0.5)).reshape(images, patch_count, heads)
    scores = jnp.where(iota((images, patch_count, heads), 1) < valid, scores, -1e30)
    scores = jnp.exp(scores - jnp.max(scores, axis=1, keepdims=True))
    attend = scores / jnp.sum(scores, axis=1, keepdims=True)
    attend = attend.reshape(rows, heads).astype(jnp.bfloat16)
    pooled = []
    for c in range(CHUNKS):
        copies[CHUNKS + c].wait()
        at = slice(c * block, (c + 1) * block)
        values = dot(flat, value_ref[:, at]).astype(jnp.bfloat16).astype(jnp.float32)
        terms = dot(attend, own[:, at]) * values
        terms = jnp.sum(terms.reshape(images, patch_count, block), axis=1)
        pooled.append(terms.astype(jnp.bfloat16).astype(jnp.float32))
    square = sum(jnp.sum(p * p, axis=-1, keepdims=True) for p in pooled)
    length = jnp.sqrt(square + 1e-06)
    for c in range(CHUNKS):
        at = slice(c * block, (c + 1) * block)
        out_ref[images:, at] = (pooled[c] / length).astype(jnp.bfloat16)


def pair_kernel(
    images, near_ref, far_ref, scale_hbm, bias_hbm, out_ref, scale_ref, bias_ref, sems
):
    near, width = near_ref.shape[0], near_ref.shape[1] - LANES
    far = far_ref.shape[0]
    copies = [
        pltpu.make_async_copy(scale_hbm, scale_ref, sems.at[0]),
        pltpu.make_async_copy(bias_hbm, bias_ref, sems.at[1]),
    ]
    for copy in copies:
        copy.start()
    raw = row_dot(near_ref[:, :width], far_ref[:, :width])
    match = row_dot(near_ref[:, width:], far_ref[:, width:])
    sign = jnp.where(match > 1.5, 1.0, -1.0)
    for copy in copies:
        copy.wait()
    scale, bias = scale_ref[0], bias_ref[0]
    logits = -sign * (scale * raw + bias)
    small = jnp.exp(-jnp.abs(logits))
    softplus = jnp.maximum(logits, 0.0) + jnp.log1p(small)
    slope = -sign * (jnp.where(logits >= 0.0, 1.0, small) / (1.0 + small))
    far_is_text = (iota((near, far), 1) & images) == 0
    loss = jnp.sum(jnp.where(far_is_text, softplus, 0.0), axis=-1, keepdims=True)
    slope = jnp.where(far_is_text, 0.0, slope)
    blocks = near // (2 * images)
    slope = slope.reshape(blocks, 2 * images, far)[:, :images].reshape(blocks * images, far)
    loss = loss.reshape(blocks, 2 * images, 1)[:, images:].reshape(blocks * images, 1)
    high = slope.astype(jnp.bfloat16)
    low = (slope - high.astype(jnp.float32)).astype(jnp.bfloat16)
    grad = dot(high, far_ref[:, :width]) + dot(low, far_ref[:, :width])
    out_ref[:, :width] = (scale * grad).astype(jnp.bfloat16)
    lane = iota((blocks * images, LANES), 1)
    parts = jnp.zeros((blocks * images, LANES), jnp.float32)
    for n in range(3):
        part = loss.astype(jnp.bfloat16).astype(jnp.float32)
        parts = jnp.where(lane == n, part, parts)
        loss = loss - part
    out_ref[:, width:] = parts.astype(jnp.bfloat16)


def grad_kernel(terms_ref, text_ref, loss_ref, grad_ref):
    images, width = text_ref.shape
    terms = terms_ref[...].astype(jnp.float32).reshape(NEAR, images, width + LANES)
    terms = jnp.sum(terms, axis=0)
    loss = jnp.sum(terms[:, width:], axis=-1, keepdims=True)
    diagonal = iota((images, images), 0) == iota((images, images), 1)
    loss_ref[...] = jnp.sum(jnp.where(diagonal, loss, 0.0), axis=0, keepdims=True)
    text = text_ref[...].astype(jnp.float32)
    length = jnp.sqrt(jnp.sum(text * text, axis=-1, keepdims=True) + 1e-06)
    unit = text / length
    grad = terms[:, :width]
    along = jnp.sum(grad * unit, axis=-1, keepdims=True)
    grad_ref[...] = (grad - along * unit) / length


def shards(
    wide, patches, counts, key_weight, value_weight, probe_query, text_embed, labels,
    logit_scale, logit_bias,
):
    images, _, width = patches.shape
    near = [list(range(first, first + NEAR)) for first in range(0, wide, NEAR)]
    far = [list(range(first, wide, NEAR)) for first in range(NEAR)]
    arrays = (text_embed, probe_query, patches, key_weight, value_weight)
    rows = pl.pallas_call(
        pool_kernel,
        out_shape=jax.ShapeDtypeStruct((2 * images, width + LANES), jnp.bfloat16),
        in_specs=[ANY, ANY, ANY, ANY, ANY, SMEM, SMEM],
        out_specs=VMEM,
        scratch_shapes=[pltpu.VMEM(a.shape, a.dtype) for a in arrays]
        + [pltpu.SemaphoreType.DMA((2 * CHUNKS + 3,))],
        compiler_params=pltpu.CompilerParams(vmem_limit_bytes=60 * 2**20),
        name="pool_rows",
    )(*arrays, counts, labels)
    near_rows = lax.all_gather(rows, "wide", axis=0, tiled=True, axis_index_groups=near)
    far_rows = lax.all_gather(rows, "wide", axis=0, tiled=True, axis_index_groups=far)
    terms = pl.pallas_call(
        functools.partial(pair_kernel, images),
        out_shape=jax.ShapeDtypeStruct((NEAR * images, width + LANES), jnp.bfloat16),
        in_specs=[VMEM, VMEM, ANY, ANY],
        out_specs=VMEM,
        scratch_shapes=[
            pltpu.SMEM((1,), jnp.float32),
            pltpu.SMEM((1,), jnp.float32),
            pltpu.SemaphoreType.DMA((2,)),
        ],
        compiler_params=pltpu.CompilerParams(vmem_limit_bytes=32 * 2**20),
        name="pair_terms",
    )(near_rows, far_rows, logit_scale.reshape(1), logit_bias.reshape(1))
    terms = lax.all_to_all(terms, "wide", 0, 0, tiled=True, axis_index_groups=near)
    row_loss, text_grad = pl.pallas_call(
        grad_kernel,
        out_shape=(
            jax.ShapeDtypeStruct((1, images), jnp.float32),
            jax.ShapeDtypeStruct((images, width), jnp.float32),
        ),
        in_specs=[VMEM, VMEM],
        out_specs=(VMEM, VMEM),
        name="text_gradient",
    )(terms, text_embed)
    return (row_loss.reshape(images), text_grad)


def solution(mesh):
    rows = P(("wide", "group"))
    return jax.shard_map(
        functools.partial(shards, mesh.shape["wide"]),
        mesh=mesh,
        in_specs=(rows, rows, P(), P(), P(), rows, rows, P(), P()),
        out_specs=(rows, rows),
        check_vma=False,
    )
```

time: 220 us -> 70.4 us (0.32)
  waiting for transfers between devices: 176 us -> 0 us
  blocking collectives: 0 us -> 58.7 us
  matrix products: 15.4 us -> 0 us
  between operations: 15.4 us -> 1.95 us
  Pallas kernels: 0 us -> 9.59 us
  local copies, waits for them, and re-layouts: 5.81 us -> 0 us
  other arithmetic: 5.7 us -> 0 us
    reduce_scatter x1 -> x0, waiting for transfers between devices: 108 us -> none  [shards(): lax.psum_scatter(logit_scale * jnp.dot(slope.T, image32, precision=lax.Pr...]
    all_gather x1 -> x0, waiting for transfers between devices: 67.3 us -> none  [shards(): lax.all_gather(text_unit, 'wide', axis=0, tiled=True)]
    all_gather x0 -> x2, blocking collectives: none -> 46.2 us  [the longest x1 26.1 us: shards(): lax.all_gather(rows, 'wide', axis=0, tiled=True, axis_index_groups=far)]
    dot_general x6 -> x0, matrix products: 15.4 us -> none  [the longest x1 3.77 us: pool_rows(): jnp.einsum('rphe,he->rhp', key_rows, probe_query, preferred_element_type=...]
    all_to_all x0 -> x1, blocking collectives: none -> 12.4 us  [shards(): lax.all_to_all(terms, 'wide', 0, 0, tiled=True, axis_index_groups=near)]
    pallas_call x0 -> x3, Pallas kernels: none -> 9.59 us  [the longest x1 6.54 us: shards(): pl.pallas_call(pool_kernel, out_shape=jax.ShapeDtypeStruct((2 * images, w...]
    reshape x2 -> x0, local copies, waits for them, and re-layouts: 5.68 us -> none  [the longest x1 2.86 us: pool_rows(): value_rows = value_rows.reshape(-1, patch_count, head_count, head_size)]
    reduce_sum x3 -> x0, other arithmetic: 2.32 us -> none  [the longest x2 1.25 us: unit_rows(): jnp.sum(embed32 * embed32, axis=-1, keepdims=True) + 1e-06]
  transfers between devices with their start and end apart: 2 -> 0, of which waited for: 2 -> 0; matrix products, arithmetic and copies ran while one was open for 8% -> 0% of each run, Pallas kernels for 0% -> 0%
where the time goes in v1:
time: 70.4 us; the launch traced here: 70.2 us
  blocking collectives  58.7 us (83%)
  Pallas kernels  9.59 us (14%)
  between operations  1.95 us (3%)
    all_gather x1, blocking collectives, shards(): lax.all_gather(rows, 'wide', axis=0, tiled=True, axis_index_groups=far)  26.1 us
    all_gather x1, blocking collectives, shards(): lax.all_gather(rows, 'wide', axis=0, tiled=True, axis_index_groups=near)  20.2 us
    all_to_all x1, blocking collectives, shards(): lax.all_to_all(terms, 'wide', 0, 0, tiled=True, axis_index_groups=near)  12.4 us
    pallas_call x1, Pallas kernels, shards(): pl.pallas_call(pool_kernel, out_shape=jax.ShapeDtypeStruct((2 * images, w...  6.54 us
    pallas_call x1, Pallas kernels, shards(): pl.pallas_call(grad_kernel, out_shape=(jax.ShapeDtypeStruct((1, images),...  1.75 us

profile of v1, /device:TPU:1, one launch (start us, length us, event | category | flops | bytes accessed | tf_op | source)
XLA Modules:
  0.0 70.2 jit_solution(7690650827601802726)
XLA Ops:
  0.6 6.5 %pool_rows.1 = bf16[32,1280]{1,0:T(8,128)(2,1)} custom-call(bf16[16,1152]{1,0:T(8,128)(2,1)} %text_ref.1, bf16[16,72]{1,0:T(8,128)(2,1)} %query_hbm.1, bf16[16,16,1152]{2,1,0:T(8,128)(2,1)} %patches_hbm.1, bf16[1152,1152]{1,0:T(8,128)(2,1)} %key_hbm.1, bf16[1152,1152]{1,0:T(8,128)(2,1)} %value_hbm.1, s32[16]{0:T(128)} %counts_ref.1, s32[16]{0:T(128)} %labels_ref.1), custom_call_target="tpu_custom_call" | custom-call | tf_op jit(solution)/shard_map/pool_rows/pallas_call | solution.py:182
  7.2 20.2 %all_gather.6.near_ref = bf16[128,1280]{1,0:T(8,128)(2,1)S(1)} all-gather(bf16[32,1280]{1,0:T(8,128)(2,1)} %pool_rows.1), channel_id=1, replica_groups={{0,32,64,96},{128,160,192,224},{256,288,320,352},{384,416,448,480},{512..., dimensions={0}, use_global_device_ids=true | all-gather | bytes 409600 | tf_op jit(solution)/shard_map/all_gather | solution.py:192
  27.3 26.1 %all_gather.7.far_ref = bf16[256,1280]{1,0:T(8,128)(2,1)S(1)} all-gather(bf16[32,1280]{1,0:T(8,128)(2,1)} %pool_rows.1), channel_id=1, replica_groups={{0,128,256,384,512,640,768,896},{32,160,288,416,544,672,800,928},{64,19..., dimensions={0}, use_global_device_ids=true | all-gather | bytes 737280 | tf_op jit(solution)/shard_map/all_gather | solution.py:193
  54.7 1.3 %pair_terms.1 = bf16[64,1280]{1,0:T(8,128)(2,1)S(1)} custom-call(bf16[128,1280]{1,0:T(8,128)(2,1)S(1)} %all_gather.6.near_ref, bf16[256,1280]{1,0:T(8,128)(2,1)S(1)} %all_gather.7.far_ref, f32[1]{0:T(128)} %bitcast.5.scale_hbm, f32[1]{0:T(128)} %bitcast.6.bias_hbm), custom_call_target="tpu_custom_call" | custom-call | tf_op jit(solution)/shard_map/pair_terms/pallas_call | solution.py:194
  56.0 12.4 %all_to_all.11 = bf16[4,16,1280]{2,1,0:T(8,128)(2,1)} all-to-all(bf16[4,16,1280]{2,1,0:T(8,128)(2,1)S(1)} %bitcast.7), channel_id=1, replica_groups={{0,32,64,96},{128,160,192,224},{256,288,320,352},{384,416,448,480},{512..., dimensions={0} | all-to-all | bytes 327680 | tf_op jit(solution)/shard_map/all_to_all | solution.py:207
  68.5 1.7 %text_gradient.1 = (f32[1,16]{1,0:T(1,128)}, f32[16,1152]{1,0:T(8,128)}) custom-call(bf16[64,1280]{1,0:T(8,128)(2,1)} %bitcast.8, bf16[16,1152]{1,0:T(8,128)(2,1)} %text_ref.1), custom_call_target="tpu_custom_call" | custom-call | tf_op jit(solution)/shard_map/text_gradient/pallas_call | solution.py:208

commit v2 on v1

v2 whole, which is shorter than its diff:
```python
import functools

import jax
import jax.numpy as jnp
from jax import lax
from jax.experimental import pallas as pl
from jax.experimental.pallas import tpu as pltpu
from jax.sharding import PartitionSpec as P

LANES = 128
CORES = 2
NEAR = 4

VMEM = pl.BlockSpec(memory_space=pltpu.VMEM)
ANY = pl.BlockSpec(memory_space=pl.ANY)


def dot(left, right):
    return jnp.dot(left, right, preferred_element_type=jnp.float32)


def row_dot(left, right):
    return lax.dot_general(
        left, right, (((1,), (1,)), ((), ())), preferred_element_type=jnp.float32
    )


def iota(shape, dim):
    return lax.broadcasted_iota(jnp.int32, shape, dim)


def fetch(sources, targets, sems):
    copies = [
        pltpu.make_async_copy(source, target, sems.at[n])
        for n, (source, target) in enumerate(zip(sources, targets))
    ]
    for copy in copies:
        copy.start()
    return copies


def pool_kernel(*refs):
    inputs, out_ref, scratch = refs[:7], refs[7], refs[8:]
    copies = fetch(inputs, scratch[:7], scratch[7])
    patches_ref, key_ref, value_ref, counts_ref, labels_ref, query_ref, text_ref = scratch[:7]
    patches_copy, key_copy, value_copy = copies[:3]
    images, patch_count, width = patches_ref.shape
    heads, head_size = query_ref.shape
    rows = images * patch_count

    for copy in copies[3:]:
        copy.wait()
    text = text_ref[...].astype(jnp.float32)
    length = jnp.sqrt(jnp.sum(text * text, axis=-1, keepdims=True) + 1e-06)
    out_ref[0:images, 0:width] = (text / length).astype(jnp.bfloat16)
    wide = lax.axis_index("wide")
    lane = iota((images, LANES), 1)
    row = iota((images, LANES), 0)
    place = (lane == wide) | (lane == row + 32)
    out_ref[0:images, width:] = jnp.where(place, 1.0, 0.0).astype(jnp.bfloat16)
    first = jnp.zeros((images, LANES), jnp.int32)
    second = jnp.zeros((images, LANES), jnp.int32)
    valid = jnp.zeros((images, patch_count, heads), jnp.int32)
    image = iota((images, patch_count, heads), 0)
    for i in range(images):
        label = labels_ref[i]
        high = lax.shift_right_logical(label, 4)
        first = jnp.where(row == i, high, first)
        second = jnp.where(row == i, label - 16 * high + 32, second)
        valid = jnp.where(image == i, counts_ref[i], valid)
    place = (lane == first) | (lane == second)
    out_ref[images:, width:] = jnp.where(place, 1.0, 0.0).astype(jnp.bfloat16)
    valid = iota((images, patch_count, heads), 1) < valid

    column = iota((1, width), 1)
    head_of = jnp.zeros((1, width), jnp.int32)
    for h in range(1, heads):
        head_of += (column >= h * head_size).astype(jnp.int32)
    inner = column - head_of * head_size
    spread = jnp.where(iota((head_size, width), 0) == inner, 1.0, 0.0).astype(jnp.bfloat16)
    own = iota((heads, width), 0) == head_of
    query = jnp.where(own, dot(query_ref[...], spread), 0.0).astype(jnp.bfloat16)
    own = jnp.where(own, 1.0, 0.0).astype(jnp.bfloat16)

    patches_copy.wait()
    flat = patches_ref[...].reshape(rows, width)
    key_copy.wait()
    keys = dot(flat, key_ref[...]).astype(jnp.bfloat16)
    scores = row_dot(keys, query)
    value_copy.wait()
    values = dot(flat, value_ref[...]).astype(jnp.bfloat16)
    scores = (scores * (1.0 / head_size**0.5)).reshape(images, patch_count, heads)
    scores = jnp.where(valid, scores, -1e30)
    scores = jnp.exp(scores - jnp.max(scores, axis=1, keepdims=True))
    attend = scores / jnp.sum(scores, axis=1, keepdims=True)
    attend = attend.reshape(rows, heads).astype(jnp.bfloat16)
    terms = dot(attend, own) * values.astype(jnp.float32)
    pooled = jnp.sum(terms.reshape(images, patch_count, width), axis=1)
    pooled = pooled.astype(jnp.bfloat16).astype(jnp.float32)
    length = jnp.sqrt(jnp.sum(pooled * pooled, axis=-1, keepdims=True) + 1e-06)
    out_ref[images:, 0:width] = (pooled / length).astype(jnp.bfloat16)


def pair_kernel(
    images, own_ref, first_ref, second_ref, third_ref, far_ref, scalar_hbm, out_ref,
    scalar_ref, sems,
):
    copy = fetch([scalar_hbm], [scalar_ref], sems)[0]
    near_rows = jnp.concatenate(
        [own_ref[...], first_ref[...], second_ref[...], third_ref[...]], axis=0
    )
    near, width = near_rows.shape[0], near_rows.shape[1] - LANES
    far = far_ref.shape[0]
    raw = row_dot(near_rows[:, :width], far_ref[:, :width])
    match = row_dot(near_rows[:, width:], far_ref[:, width:])
    sign = jnp.where(match > 1.5, 1.0, -1.0)
    copy.wait()
    scale, bias = scalar_ref[0], scalar_ref[1]
    logits = -sign * (scale * raw + bias)
    small = jnp.exp(-jnp.abs(logits))
    softplus = jnp.maximum(logits, 0.0) + jnp.log1p(small)
    slope = -sign * (jnp.where(logits >= 0.0, 1.0, small) / (1.0 + small))
    far_is_text = (iota((near, far), 1) & images) == 0
    loss = jnp.sum(jnp.where(far_is_text, softplus, 0.0), axis=-1, keepdims=True)
    slope = jnp.where(far_is_text, 0.0, slope)
    slope = slope.reshape(NEAR, 2 * images, far)[:, :images].reshape(NEAR * images, far)
    loss = loss.reshape(NEAR, 2 * images, 1)[:, images:].reshape(NEAR * images, 1)
    high = slope.astype(jnp.bfloat16)
    low = (slope - high.astype(jnp.float32)).astype(jnp.bfloat16)
    grad = scale * (dot(high, far_ref[:, :width]) + dot(low, far_ref[:, :width]))
    lane = iota((NEAR * images, LANES), 1)
    parts = jnp.zeros((NEAR * images, LANES), jnp.float32)
    for n in range(3):
        part = loss.astype(jnp.bfloat16).astype(jnp.float32)
        parts = jnp.where(lane == n, part, parts)
        loss = loss - part
    place = own_ref[0:1, width:].astype(jnp.float32).astype(jnp.int32)
    lane = iota((1, LANES), 1)
    place = jnp.sum(jnp.where(lane < 32, place * lane, 0), axis=-1, keepdims=True)
    place = lax.shift_right_logical(place, 1) & (NEAR - 1)
    for target in range(NEAR):
        at = slice(target * images, (target + 1) * images)
        for source, columns in ((grad, slice(0, width)), (parts, slice(width, None))):
            block = source[0:images]
            for n in range(1, NEAR):
                block = jnp.where(place == (target ^ n), source[n * images : (n + 1) * images], block)
            out_ref[at, columns] = block.astype(jnp.bfloat16)


def grad_kernel(terms_ref, text_ref, loss_ref, grad_ref):
    images, width = text_ref.shape
    terms = terms_ref[...].astype(jnp.float32).reshape(NEAR, images, width + LANES)
    terms = jnp.sum(terms, axis=0)
    loss = jnp.sum(terms[:, width:], axis=-1, keepdims=True)
    diagonal = iota((images, images), 0) == iota((images, images), 1)
    loss_ref[...] = jnp.sum(jnp.where(diagonal, loss, 0.0), axis=0, keepdims=True)
    text = text_ref[...].astype(jnp.float32)
    length = jnp.sqrt(jnp.sum(text * text, axis=-1, keepdims=True) + 1e-06)
    unit = text / length
    grad = terms[:, :width]
    along = jnp.sum(grad * unit, axis=-1, keepdims=True)
    grad_ref[...] = (grad - along * unit) / length


def shards(
    wide, patches, counts, key_weight, value_weight, probe_query, text_embed, labels,
    logit_scale, logit_bias,
):
    images, _, width = patches.shape
    block = NEAR * CORES
    near = [
        [first + core + CORES * chip for chip in range(NEAR)]
        for first in range(0, wide, block)
        for core in range(CORES)
    ]
    far = [
        [first + CORES * chip + core for first in range(0, wide, block) for core in range(CORES)]
        for chip in range(NEAR)
    ]
    arrays = (patches, key_weight, value_weight, counts, labels, probe_query, text_embed)
    places = (pltpu.VMEM,) * 3 + (pltpu.SMEM,) * 2 + (pltpu.VMEM,) * 2
    rows = pl.pallas_call(
        pool_kernel,
        out_shape=jax.ShapeDtypeStruct((2 * images, width + LANES), jnp.bfloat16),
        in_specs=[ANY] * 7,
        out_specs=VMEM,
        scratch_shapes=[place(a.shape, a.dtype) for place, a in zip(places, arrays)]
        + [pltpu.SemaphoreType.DMA((7,))],
        compiler_params=pltpu.CompilerParams(vmem_limit_bytes=60 * 2**20),
        name="pool_rows",
    )(*arrays)
    near_rows = [
        lax.ppermute(rows, "wide", [(i, i ^ (CORES * n)) for i in range(wide)])
        for n in range(1, NEAR)
    ]
    far_rows = lax.all_gather(rows, "wide", axis=0, tiled=True, axis_index_groups=far)
    terms = pl.pallas_call(
        functools.partial(pair_kernel, images),
        out_shape=jax.ShapeDtypeStruct((NEAR * images, width + LANES), jnp.bfloat16),
        in_specs=[VMEM] * 5 + [ANY],
        out_specs=VMEM,
        scratch_shapes=[pltpu.SMEM((2,), jnp.float32), pltpu.SemaphoreType.DMA((1,))],
        compiler_params=pltpu.CompilerParams(vmem_limit_bytes=32 * 2**20),
        name="pair_terms",
    )(rows, *near_rows, far_rows, jnp.stack([logit_scale, logit_bias]))
    terms = lax.all_to_all(terms, "wide", 0, 0, tiled=True, axis_index_groups=near)
    row_loss, text_grad = pl.pallas_call(
        grad_kernel,
        out_shape=(
            jax.ShapeDtypeStruct((1, images), jnp.float32),
            jax.ShapeDtypeStruct((images, width), jnp.float32),
        ),
        in_specs=[VMEM, VMEM],
        out_specs=(VMEM, VMEM),
        name="text_gradient",
    )(terms, text_embed)
    return (row_loss.reshape(images), text_grad)


def solution(mesh):
    rows = P(("wide", "group"))
    return jax.shard_map(
        functools.partial(shards, mesh.shape["wide"]),
        mesh=mesh,
        in_specs=(rows, rows, P(), P(), P(), rows, rows, P(), P()),
        out_specs=(rows, rows),
        check_vma=False,
    )
```

time: 70.4 us -> 67.8 us (0.963)
  blocking collectives: 58.7 us -> 43 us
  starting transfers between devices: 0 us -> 12.6 us
  local copies, waits for them, and re-layouts: 0 us -> 0.88 us
  Pallas kernels: 9.59 us -> 8.81 us
    all_gather x1 -> x0, blocking collectives: 20.2 us -> none  [shards(): lax.all_gather(rows, 'wide', axis=0, tiled=True, axis_index_groups=near)]
    ppermute x0 -> x3, starting transfers between devices: none -> 12.6 us  [shards(): lax.ppermute(rows, 'wide', [(i, i ^ CORES * n) for i in range(wide)])]
    all_gather x1, blocking collectives: 26.1 us -> 33 us  [shards(): lax.all_gather(rows, 'wide', axis=0, tiled=True, axis_index_groups=far)]
    all_to_all x1, blocking collectives: 12.4 us -> 9.99 us  [shards(): lax.all_to_all(terms, 'wide', 0, 0, tiled=True, axis_index_groups=near)]
    unnamed x0 -> x2, local copies, waits for them, and re-layouts: none -> 0.88 us
  transfers between devices with their start and end apart: 0 -> 3, of which waited for: 0 -> 0; matrix products, arithmetic and copies ran while one was open for 0% -> 0% of each run, Pallas kernels for 0% -> 0%
where the time goes in v2:
time: 67.8 us; the launch traced here: 67.3 us
  blocking collectives  43 us (63%)
  starting transfers between devices  12.6 us (19%)
  Pallas kernels  8.81 us (13%)
  between operations  1.98 us (3%)
  local copies, waits for them, and re-layouts  0.88 us (1%)
    all_gather x1, blocking collectives, shards(): lax.all_gather(rows, 'wide', axis=0, tiled=True, axis_index_groups=far)  33 us
    ppermute x3, starting transfers between devices, shards(): lax.ppermute(rows, 'wide', [(i, i ^ CORES * n) for i in range(wide)])  12.6 us
    all_to_all x1, blocking collectives, shards(): lax.all_to_all(terms, 'wide', 0, 0, tiled=True, axis_index_groups=near)  9.99 us
    pallas_call x1, Pallas kernels, shards(): pl.pallas_call(pool_kernel, out_shape=jax.ShapeDtypeStruct((2 * images, w...  6.06 us
    pallas_call x1, Pallas kernels, shards(): pl.pallas_call(grad_kernel, out_shape=(jax.ShapeDtypeStruct((1, images),...  1.75 us
  transfers between devices with their start and end apart: 3, of which 0 were waited for; matrix products, arithmetic and copies ran while one was open for 0% of the time, Pallas kernels for 0%

profile of v2, /device:TPU:1, one launch (start us, length us, event | category | flops | bytes accessed | tf_op | source)
XLA Modules:
  0.0 67.3 jit_solution(4055074985155606181)
XLA Ops:
  0.6 6.1 %pool_rows.1.own_ref = bf16[32,1280]{1,0:T(8,128)(2,1)} custom-call(bf16[16,16,1152]{2,1,0:T(8,128)(2,1)} %refs_0_.1, bf16[1152,1152]{1,0:T(8,128)(2,1)} %refs_1_.1, bf16[1152,1152]{1,0:T(8,128)(2,1)} %refs_2_.1, s32[16]{0:T(128)} %refs_3_.1, s32[16]{0:T(128)} %refs_4_.1, bf16[16,72]{1,0:T(8,128)(2,1)} %refs_5_.1, bf16[16,1152]{1,0:T(8,128)(2,1)} %text_ref.1), custom_call_target="tpu_custom_call" | custom-call | tf_op jit(solution)/shard_map/pool_rows/pallas_call | solution.py:182
  6.7 8.4 %collective-permute-start.2 = (bf16[32,1280]{1,0:T(8,128)(2,1)}, bf16[32,1280]{1,0:T(8,128)(2,1)S(1)}, u32[]{:S(2)}, u32[]{:S(2)}) collective-permute-start(bf16[32,1280]{1,0:T(8,128)(2,1)} %pool_rows.1.own_ref), channel_id=1, source_target_pairs={{0,192},{32,224},{64,128},{96,160},{128,64},{160,96},{192,0},{224,... | collective-permute-start | bytes 245768 | tf_op jit(solution)/shard_map/ppermute | solution.py:193
  15.2 1.9 %collective-permute-start.1 = (bf16[32,1280]{1,0:T(8,128)(2,1)}, bf16[32,1280]{1,0:T(8,128)(2,1)S(1)}, u32[]{:S(2)}, u32[]{:S(2)}) collective-permute-start(bf16[32,1280]{1,0:T(8,128)(2,1)} %pool_rows.1.own_ref), channel_id=1, source_target_pairs={{0,128},{32,160},{64,192},{96,224},{128,0},{160,32},{192,64},{224,... | collective-permute-start | bytes 245768 | tf_op jit(solution)/shard_map/ppermute | solution.py:193
  17.1 2.2 %collective-permute-start = (bf16[32,1280]{1,0:T(8,128)(2,1)}, bf16[32,1280]{1,0:T(8,128)(2,1)S(1)}, u32[]{:S(2)}, u32[]{:S(2)}) collective-permute-start(bf16[32,1280]{1,0:T(8,128)(2,1)} %pool_rows.1.own_ref), channel_id=1, source_target_pairs={{0,64},{32,96},{64,0},{96,32},{128,192},{160,224},{192,128},{224,1... | collective-permute-start | bytes 245768 | tf_op jit(solution)/shard_map/ppermute | solution.py:193
  19.3 33.0 %all_gather.3.far_ref = bf16[256,1280]{1,0:T(8,128)(2,1)S(1)} all-gather(bf16[32,1280]{1,0:T(8,128)(2,1)} %pool_rows.1.own_ref), channel_id=1, replica_groups={{0,32,256,288,512,544,768,800},{64,96,320,352,576,608,832,864},{128,160..., dimensions={0}, use_global_device_ids=true | all-gather | bytes 737280 | tf_op jit(solution)/shard_map/all_gather | solution.py:196
  53.5 0.1 pad_maximum_fusion.scalar_hbm
  53.6 0.0 collective-permute-done.2.third_ref
  53.6 0.0 collective-permute-done.1.second_ref
  53.6 0.0 collective-permute-done.first_ref
  53.6 0.0 copy-start
  53.6 0.9 %copy-done = bf16[32,1280]{1,0:T(8,128)(2,1)S(1)} copy-done((bf16[32,1280]{1,0:T(8,128)(2,1)S(1)}, bf16[32,1280]{1,0:T(8,128)(2,1)}, u32[]{:S(2)}) %copy-start) | copy-done | bytes 81944
  54.5 1.0 %pair_terms.1 = bf16[64,1280]{1,0:T(8,128)(2,1)S(1)} custom-call(bf16[32,1280]{1,0:T(8,128)(2,1)S(1)} %copy-done, bf16[32,1280]{1,0:T(8,128)(2,1)S(1)} %collective-permute-done.first_ref, bf16[32,1280]{1,0:T(8,128)(2,1)S(1)} %collective-permute-done.1.second_ref, bf16[32,1280]{1,0:T(8,128)(2,1)S(1)} %collective-permute-done.2.third_ref, ...), custom_call_target="tpu_custom_call" | custom-call | tf_op jit(solution)/shard_map/pair_terms/pallas_call | solution.py:197
  55.5 10.0 %all_to_all.11 = bf16[4,16,1280]{2,1,0:T(8,128)(2,1)} all-to-all(bf16[4,16,1280]{2,1,0:T(8,128)(2,1)S(1)} %bitcast.7), channel_id=1, replica_groups={{0,64,128,192},{32,96,160,224},{256,320,384,448},{288,352,416,480},{512..., dimensions={0} | all-to-all | bytes 327680 | tf_op jit(solution)/shard_map/all_to_all | solution.py:206
  65.5 1.7 %text_gradient.1 = (f32[1,16]{1,0:T(1,128)}, f32[16,1152]{1,0:T(8,128)}) custom-call(bf16[64,1280]{1,0:T(8,128)(2,1)} %bitcast.8, bf16[16,1152]{1,0:T(8,128)(2,1)} %text_ref.1), custom_call_target="tpu_custom_call" | custom-call | tf_op jit(solution)/shard_map/text_gradient/pallas_call | solution.py:207
Async XLA Ops:
  6.7 46.9 %collective-permute-start.2 = (bf16[32,1280]{1,0:T(8,128)(2,1)}, bf16[32,1280]{1,0:T(8,128)(2,1)S(1)}, u32[]{:S(2)}, u32[]{:S(2)}) collective-permute-start(bf16[32,1280]{1,0:T(8,128)(2,1)} %pool_rows.1.own_ref), channel_id=1, source_target_pairs={{0,192},{32,224},{64,128},{96,160},{128,64},{160,96},{192,0},{224,... | collective-permute-start | bytes 245768 | tf_op jit(solution)/shard_map/ppermute | solution.py:193
  15.2 38.5 %collective-permute-start.1 = (bf16[32,1280]{1,0:T(8,128)(2,1)}, bf16[32,1280]{1,0:T(8,128)(2,1)S(1)}, u32[]{:S(2)}, u32[]{:S(2)}) collective-permute-start(bf16[32,1280]{1,0:T(8,128)(2,1)} %pool_rows.1.own_ref), channel_id=1, source_target_pairs={{0,128},{32,160},{64,192},{96,224},{128,0},{160,32},{192,64},{224,... | collective-permute-start | bytes 245768 | tf_op jit(solution)/shard_map/ppermute | solution.py:193
  17.1 36.6 %collective-permute-start = (bf16[32,1280]{1,0:T(8,128)(2,1)}, bf16[32,1280]{1,0:T(8,128)(2,1)S(1)}, u32[]{:S(2)}, u32[]{:S(2)}) collective-permute-start(bf16[32,1280]{1,0:T(8,128)(2,1)} %pool_rows.1.own_ref), channel_id=1, source_target_pairs={{0,64},{32,96},{64,0},{96,32},{128,192},{160,224},{192,128},{224,1... | collective-permute-start | bytes 245768 | tf_op jit(solution)/shard_map/ppermute | solution.py:193
  53.6 0.9 %copy-start = (bf16[32,1280]{1,0:T(8,128)(2,1)S(1)}, bf16[32,1280]{1,0:T(8,128)(2,1)}, u32[]{:S(2)}) copy-start(bf16[32,1280]{1,0:T(8,128)(2,1)} %pool_rows.1.own_ref) | copy-start | bytes 245764

commit v3 on v2

--- a/solution.py
+++ b/solution.py
@@ -12,6 +12,7 @@
 NEAR = 4
 
 VMEM = pl.BlockSpec(memory_space=pltpu.VMEM)
+SMEM = pl.BlockSpec(memory_space=pltpu.SMEM)
 ANY = pl.BlockSpec(memory_space=pl.ANY)
 
 
@@ -29,27 +30,37 @@
     return lax.broadcasted_iota(jnp.int32, shape, dim)
 
 
-def fetch(sources, targets, sems):
-    copies = [
-        pltpu.make_async_copy(source, target, sems.at[n])
-        for n, (source, target) in enumerate(zip(sources, targets))
-    ]
+def start(copies):
     for copy in copies:
         copy.start()
-    return copies
+
+
+def wait(copies):
+    for copy in copies:
+        copy.wait()
 
 
 def pool_kernel(*refs):
     inputs, out_ref, scratch = refs[:7], refs[7], refs[8:]
-    copies = fetch(inputs, scratch[:7], scratch[7])
     patches_ref, key_ref, value_ref, counts_ref, labels_ref, query_ref, text_ref = scratch[:7]
-    patches_copy, key_copy, value_copy = copies[:3]
+    sems = scratch[7]
     images, patch_count, width = patches_ref.shape
     heads, head_size = query_ref.shape
     rows = images * patch_count
-
-    for copy in copies[3:]:
-        copy.wait()
+    copies = [
+        pltpu.make_async_copy(source, target, sems.at[n])
+        for n, (source, target) in enumerate(zip(inputs, scratch[:7]))
+    ]
+    patches_copy, value_copy, small_copies = copies[0], copies[2], copies[3:]
+    cut = width // (2 * LANES) * LANES + LANES
+    key_parts = [slice(0, cut), slice(cut, width)]
+    key_copies = [
+        pltpu.make_async_copy(inputs[1].at[:, at], key_ref.at[:, at], sems.at[n])
+        for n, at in zip((1, 7), key_parts)
+    ]
+    start(small_copies + [patches_copy] + key_copies)
+    wait(small_copies)
+    value_copy.start()
     text = text_ref[...].astype(jnp.float32)
     length = jnp.sqrt(jnp.sum(text * text, axis=-1, keepdims=True) + 1e-06)
     out_ref[0:images, 0:width] = (text / length).astype(jnp.bfloat16)
@@ -84,9 +95,11 @@
 
     patches_copy.wait()
     flat = patches_ref[...].reshape(rows, width)
-    key_copy.wait()
-    keys = dot(flat, key_ref[...]).astype(jnp.bfloat16)
-    scores = row_dot(keys, query)
+    scores = jnp.zeros((rows, heads), jnp.float32)
+    for at, copy in zip(key_parts, key_copies):
+        copy.wait()
+        keys = dot(flat, key_ref[:, at]).astype(jnp.bfloat16)
+        scores += row_dot(keys, query[:, at])
     value_copy.wait()
     values = dot(flat, value_ref[...]).astype(jnp.bfloat16)
     scores = (scores * (1.0 / head_size**0.5)).reshape(images, patch_count, heads)
@@ -102,20 +115,15 @@
 
 
 def pair_kernel(
-    images, own_ref, first_ref, second_ref, third_ref, far_ref, scalar_hbm, out_ref,
-    scalar_ref, sems,
+    images, pair_ref, other_ref, far_ref, scale_ref, bias_ref, out_ref
 ):
-    copy = fetch([scalar_hbm], [scalar_ref], sems)[0]
-    near_rows = jnp.concatenate(
-        [own_ref[...], first_ref[...], second_ref[...], third_ref[...]], axis=0
-    )
+    near_rows = jnp.concatenate([pair_ref[...], other_ref[...]], axis=0)
     near, width = near_rows.shape[0], near_rows.shape[1] - LANES
     far = far_ref.shape[0]
     raw = row_dot(near_rows[:, :width], far_ref[:, :width])
     match = row_dot(near_rows[:, width:], far_ref[:, width:])
     sign = jnp.where(match > 1.5, 1.0, -1.0)
-    copy.wait()
-    scale, bias = scalar_ref[0], scalar_ref[1]
+    scale, bias = scale_ref[0], bias_ref[0]
     logits = -sign * (scale * raw + bias)
     small = jnp.exp(-jnp.abs(logits))
     softplus = jnp.maximum(logits, 0.0) + jnp.log1p(small)
@@ -134,17 +142,15 @@
         part = loss.astype(jnp.bfloat16).astype(jnp.float32)
         parts = jnp.where(lane == n, part, parts)
         loss = loss - part
-    place = own_ref[0:1, width:].astype(jnp.float32).astype(jnp.int32)
+    place = pair_ref[0:1, width:].astype(jnp.float32).astype(jnp.int32)
     lane = iota((1, LANES), 1)
     place = jnp.sum(jnp.where(lane < 32, place * lane, 0), axis=-1, keepdims=True)
-    place = lax.shift_right_logical(place, 1) & (NEAR - 1)
-    for target in range(NEAR):
-        at = slice(target * images, (target + 1) * images)
-        for source, columns in ((grad, slice(0, width)), (parts, slice(width, None))):
-            block = source[0:images]
-            for n in range(1, NEAR):
-                block = jnp.where(place == (target ^ n), source[n * images : (n + 1) * images], block)
-            out_ref[at, columns] = block.astype(jnp.bfloat16)
+    second = (place & (CORES * NEAR // 2)) != 0
+    half = NEAR // 2 * images
+    for source, columns in ((grad, slice(0, width)), (parts, slice(width, None))):
+        low, high = source[:half], source[half:]
+        out_ref[:half, columns] = jnp.where(second, high, low).astype(jnp.bfloat16)
+        out_ref[half:, columns] = jnp.where(second, low, high).astype(jnp.bfloat16)
 
 
 def grad_kernel(terms_ref, text_ref, loss_ref, grad_ref):
@@ -173,6 +179,11 @@
         for first in range(0, wide, block)
         for core in range(CORES)
     ]
+    pairs = [
+        [first + core, first + CORES + core]
+        for first in range(0, wide, 2 * CORES)
+        for core in range(CORES)
+    ]
     far = [
         [first + CORES * chip + core for first in range(0, wide, block) for core in range(CORES)]
         for chip in range(NEAR)
@@ -185,24 +196,21 @@
         in_specs=[ANY] * 7,
         out_specs=VMEM,
         scratch_shapes=[place(a.shape, a.dtype) for place, a in zip(places, arrays)]
-        + [pltpu.SemaphoreType.DMA((7,))],
+        + [pltpu.SemaphoreType.DMA((8,))],
         compiler_params=pltpu.CompilerParams(vmem_limit_bytes=60 * 2**20),
         name="pool_rows",
     )(*arrays)
-    near_rows = [
-        lax.ppermute(rows, "wide", [(i, i ^ (CORES * n)) for i in range(wide)])
-        for n in range(1, NEAR)
-    ]
+    pair_rows = lax.all_gather(rows, "wide", axis=0, tiled=True, axis_index_groups=pairs)
+    other_rows = lax.ppermute(pair_rows, "wide", [(i, i ^ block // 2) for i in range(wide)])
     far_rows = lax.all_gather(rows, "wide", axis=0, tiled=True, axis_index_groups=far)
     terms = pl.pallas_call(
         functools.partial(pair_kernel, images),
         out_shape=jax.ShapeDtypeStruct((NEAR * images, width + LANES), jnp.bfloat16),
-        in_specs=[VMEM] * 5 + [ANY],
+        in_specs=[VMEM] * 3 + [SMEM] * 2,
         out_specs=VMEM,
-        scratch_shapes=[pltpu.SMEM((2,), jnp.float32), pltpu.SemaphoreType.DMA((1,))],
         compiler_params=pltpu.CompilerParams(vmem_limit_bytes=32 * 2**20),
         name="pair_terms",
-    )(rows, *near_rows, far_rows, jnp.stack([logit_scale, logit_bias]))
+    )(pair_rows, other_rows, far_rows, logit_scale.reshape(1), logit_bias.reshape(1))
     terms = lax.all_to_all(terms, "wide", 0, 0, tiled=True, axis_index_groups=near)
     row_loss, text_grad = pl.pallas_call(
         grad_kernel,

time: 67.8 us -> 65.4 us (0.965)
  starting transfers between devices: 12.6 us -> 6.14 us
  blocking collectives: 43 us -> 49.3 us
  Pallas kernels: 8.81 us -> 7.8 us
  local copies, waits for them, and re-layouts: 0.88 us -> 0 us
    ppermute x3 -> x1, starting transfers between devices: 12.6 us -> 6.14 us  [shards(): lax.ppermute(pair_rows, 'wide', [(i, i ^ block // 2) for i in range(wide)])]
    all_gather x0 -> x1, blocking collectives: none -> 5.68 us  [shards(): lax.all_gather(rows, 'wide', axis=0, tiled=True, axis_index_groups=pairs)]
    all_to_all x1, blocking collectives: 9.99 us -> 13 us  [shards(): lax.all_to_all(terms, 'wide', 0, 0, tiled=True, axis_index_groups=near)]
    all_gather x1, blocking collectives: 33 us -> 30.6 us  [shards(): lax.all_gather(rows, 'wide', axis=0, tiled=True, axis_index_groups=far)]
    pallas_call x1, Pallas kernels: 6.06 us -> 5.16 us  [shards(): pl.pallas_call(pool_kernel, out_shape=jax.ShapeDtypeStruct((2 * images, w...]
    unnamed x2 -> x0, local copies, waits for them, and re-layouts: 0.88 us -> none
  transfers between devices with their start and end apart: 3 -> 1, of which waited for: 0 -> 0; matrix products, arithmetic and copies ran while one was open for 0% -> 0% of each run, Pallas kernels for 0% -> 0%
where the time goes in v3:
time: 65.4 us; the launch traced here: 65.2 us
  blocking collectives  49.3 us (75%)
  Pallas kernels  7.8 us (12%)
  starting transfers between devices  6.14 us (9%)
  between operations  1.95 us (3%)
    all_gather x1, blocking collectives, shards(): lax.all_gather(rows, 'wide', axis=0, tiled=True, axis_index_groups=far)  30.6 us
    all_to_all x1, blocking collectives, shards(): lax.all_to_all(terms, 'wide', 0, 0, tiled=True, axis_index_groups=near)  13 us
    ppermute x1, starting transfers between devices, shards(): lax.ppermute(pair_rows, 'wide', [(i, i ^ block // 2) for i in range(wide)])  6.14 us
    all_gather x1, blocking collectives, shards(): lax.all_gather(rows, 'wide', axis=0, tiled=True, axis_index_groups=pairs)  5.68 us
    pallas_call x1, Pallas kernels, shards(): pl.pallas_call(pool_kernel, out_shape=jax.ShapeDtypeStruct((2 * images, w...  5.16 us
    pallas_call x1, Pallas kernels, shards(): pl.pallas_call(grad_kernel, out_shape=(jax.ShapeDtypeStruct((1, images),...  1.75 us
  transfers between devices with their start and end apart: 1, of which 0 were waited for; matrix products, arithmetic and copies ran while one was open for 0% of the time, Pallas kernels for 0%

profile of v3, /device:TPU:1, one launch (start us, length us, event | category | flops | bytes accessed | tf_op | source)
XLA Modules:
  0.0 65.2 jit_solution(11462265299609387327)
XLA Ops:
  0.6 5.2 %pool_rows.1 = bf16[32,1280]{1,0:T(8,128)(2,1)} custom-call(bf16[16,16,1152]{2,1,0:T(8,128)(2,1)} %refs_0_.1, bf16[1152,1152]{1,0:T(8,128)(2,1)} %refs_1_.1, bf16[1152,1152]{1,0:T(8,128)(2,1)} %refs_2_.1, s32[16]{0:T(128)} %refs_3_.1, s32[16]{0:T(128)} %refs_4_.1, bf16[16,72]{1,0:T(8,128)(2,1)} %refs_5_.1, bf16[16,1152]{1,0:T(8,128)(2,1)} %text_ref.1), custom_call_target="tpu_custom_call" | custom-call | tf_op jit(solution)/shard_map/pool_rows/pallas_call | solution.py:193
  5.8 5.7 %all_gather.6.pair_ref = bf16[64,1280]{1,0:T(8,128)(2,1)S(1)} all-gather(bf16[32,1280]{1,0:T(8,128)(2,1)} %pool_rows.1), channel_id=1, replica_groups={{0,64},{32,96},{128,192},{160,224},{256,320},{288,352},{384,448},{416,4..., dimensions={0}, use_global_device_ids=true | all-gather | bytes 245760 | tf_op jit(solution)/shard_map/all_gather | solution.py:203
  11.5 6.1 %collective-permute-start = (bf16[64,1280]{1,0:T(8,128)(2,1)S(1)}, bf16[64,1280]{1,0:T(8,128)(2,1)S(1)}, u32[]{:S(2)}, u32[]{:S(2)}) collective-permute-start(bf16[64,1280]{1,0:T(8,128)(2,1)S(1)} %all_gather.6.pair_ref), channel_id=1, source_target_pairs={{0,128},{32,160},{64,192},{96,224},{128,0},{160,32},{192,64},{224,... | collective-permute-start | bytes 491528 | tf_op jit(solution)/shard_map/ppermute | solution.py:204
  18.9 30.6 %all_gather.7.far_ref = bf16[256,1280]{1,0:T(8,128)(2,1)S(1)} all-gather(bf16[32,1280]{1,0:T(8,128)(2,1)} %pool_rows.1), channel_id=1, replica_groups={{0,32,256,288,512,544,768,800},{64,96,320,352,576,608,832,864},{128,160..., dimensions={0}, use_global_device_ids=true | all-gather | bytes 737280 | tf_op jit(solution)/shard_map/all_gather | solution.py:205
  49.5 0.0 collective-permute-done.other_ref
  49.5 0.9 %pair_terms.1 = bf16[64,1280]{1,0:T(8,128)(2,1)S(1)} custom-call(bf16[64,1280]{1,0:T(8,128)(2,1)S(1)} %all_gather.6.pair_ref, bf16[64,1280]{1,0:T(8,128)(2,1)S(1)} %collective-permute-done.other_ref, bf16[256,1280]{1,0:T(8,128)(2,1)S(1)} %all_gather.7.far_ref, f32[1]{0:T(128)} %bitcast.5.scale_ref, f32[1]{0:T(128)} %bitcast.6.bias_ref), custom_call_target="tpu_custom_call" | custom-call | tf_op jit(solution)/shard_map/pair_terms/pallas_call | solution.py:206
  50.4 13.0 %all_to_all.11 = bf16[4,16,1280]{2,1,0:T(8,128)(2,1)} all-to-all(bf16[4,16,1280]{2,1,0:T(8,128)(2,1)S(1)} %bitcast.7), channel_id=1, replica_groups={{0,64,128,192},{32,96,160,224},{256,320,384,448},{288,352,416,480},{512..., dimensions={0} | all-to-all | bytes 327680 | tf_op jit(solution)/shard_map/all_to_all | solution.py:214
  63.5 1.7 %text_gradient.1 = (f32[1,16]{1,0:T(1,128)}, f32[16,1152]{1,0:T(8,128)}) custom-call(bf16[64,1280]{1,0:T(8,128)(2,1)} %bitcast.8, bf16[16,1152]{1,0:T(8,128)(2,1)} %text_ref.1), custom_call_target="tpu_custom_call" | custom-call | tf_op jit(solution)/shard_map/text_gradient/pallas_call | solution.py:215
Async XLA Ops:
  11.5 38.1 %collective-permute-start = (bf16[64,1280]{1,0:T(8,128)(2,1)S(1)}, bf16[64,1280]{1,0:T(8,128)(2,1)S(1)}, u32[]{:S(2)}, u32[]{:S(2)}) collective-permute-start(bf16[64,1280]{1,0:T(8,128)(2,1)S(1)} %all_gather.6.pair_ref), channel_id=1, source_target_pairs={{0,128},{32,160},{64,192},{96,224},{128,0},{160,32},{192,64},{224,... | collective-permute-start | bytes 491528 | tf_op jit(solution)/shard_map/ppermute | solution.py:204

commit v4 on v3

--- a/solution.py
+++ b/solution.py
@@ -47,11 +47,9 @@
     images, patch_count, width = patches_ref.shape
     heads, head_size = query_ref.shape
     rows = images * patch_count
-    copies = [
-        pltpu.make_async_copy(source, target, sems.at[n])
-        for n, (source, target) in enumerate(zip(inputs, scratch[:7]))
-    ]
-    patches_copy, value_copy, small_copies = copies[0], copies[2], copies[3:]
+    patches_copy, value_copy, *small_copies = [
+        pltpu.make_async_copy(inputs[n], scratch[n], sems.at[n]) for n in (0, 2, 3, 4, 5, 6)
+    ]
     cut = width // (2 * LANES) * LANES + LANES
     key_parts = [slice(0, cut), slice(cut, width)]
     key_copies = [
@@ -114,16 +112,27 @@
     out_ref[images:, 0:width] = (pooled / length).astype(jnp.bfloat16)
 
 
-def pair_kernel(
-    images, pair_ref, other_ref, far_ref, scale_ref, bias_ref, out_ref
-):
-    near_rows = jnp.concatenate([pair_ref[...], other_ref[...]], axis=0)
+def pair_kernel(images, own_ref, other_ref, scale_ref, bias_ref, out_ref):
+    core = lax.axis_index("wide") & 1
+    scale, bias = scale_ref[0], bias_ref[0]
+    for this, (near_ref, far_ref) in enumerate(((own_ref, other_ref), (other_ref, own_ref))):
+        pl.when(core == this)(
+            functools.partial(
+                pair_terms, images, this, near_ref, far_ref, scale, bias, out_ref
+            )
+        )
+
+
+def pair_terms(images, core, near_ref, far_ref, scale, bias, out_ref):
+    rows = 2 * images
+    near_rows = jnp.concatenate(
+        [near_ref[pl.ds((CORES * n + core) * rows, rows)] for n in range(NEAR)]
+    )
     near, width = near_rows.shape[0], near_rows.shape[1] - LANES
     far = far_ref.shape[0]
     raw = row_dot(near_rows[:, :width], far_ref[:, :width])
     match = row_dot(near_rows[:, width:], far_ref[:, width:])
     sign = jnp.where(match > 1.5, 1.0, -1.0)
-    scale, bias = scale_ref[0], bias_ref[0]
     logits = -sign * (scale * raw + bias)
     small = jnp.exp(-jnp.abs(logits))
     softplus = jnp.maximum(logits, 0.0) + jnp.log1p(small)
@@ -142,15 +151,8 @@
         part = loss.astype(jnp.bfloat16).astype(jnp.float32)
         parts = jnp.where(lane == n, part, parts)
         loss = loss - part
-    place = pair_ref[0:1, width:].astype(jnp.float32).astype(jnp.int32)
-    lane = iota((1, LANES), 1)
-    place = jnp.sum(jnp.where(lane < 32, place * lane, 0), axis=-1, keepdims=True)
-    second = (place & (CORES * NEAR // 2)) != 0
-    half = NEAR // 2 * images
-    for source, columns in ((grad, slice(0, width)), (parts, slice(width, None))):
-        low, high = source[:half], source[half:]
-        out_ref[:half, columns] = jnp.where(second, high, low).astype(jnp.bfloat16)
-        out_ref[half:, columns] = jnp.where(second, low, high).astype(jnp.bfloat16)
+    out_ref[:, :width] = grad.astype(jnp.bfloat16)
+    out_ref[:, width:] = parts.astype(jnp.bfloat16)
 
 
 def grad_kernel(terms_ref, text_ref, loss_ref, grad_ref):
@@ -179,15 +181,11 @@
         for first in range(0, wide, block)
         for core in range(CORES)
     ]
-    pairs = [
-        [first + core, first + CORES + core]
-        for first in range(0, wide, 2 * CORES)
-        for core in range(CORES)
-    ]
+    cores = [[first, first + 1] for first in range(0, wide, CORES)]
     far = [
-        [first + CORES * chip + core for first in range(0, wide, block) for core in range(CORES)]
-        for chip in range(NEAR)
-    ]
+        [first + CORES * chip + 1 for first in range(0, wide, block)] for chip in range(NEAR)
+    ]
+    mixed = near[::CORES] + far
     arrays = (patches, key_weight, value_weight, counts, labels, probe_query, text_embed)
     places = (pltpu.VMEM,) * 3 + (pltpu.SMEM,) * 2 + (pltpu.VMEM,) * 2
     rows = pl.pallas_call(
@@ -200,17 +198,17 @@
         compiler_params=pltpu.CompilerParams(vmem_limit_bytes=60 * 2**20),
         name="pool_rows",
     )(*arrays)
-    pair_rows = lax.all_gather(rows, "wide", axis=0, tiled=True, axis_index_groups=pairs)
-    other_rows = lax.ppermute(pair_rows, "wide", [(i, i ^ block // 2) for i in range(wide)])
-    far_rows = lax.all_gather(rows, "wide", axis=0, tiled=True, axis_index_groups=far)
+    rows = lax.all_gather(rows, "wide", axis=0, tiled=True, axis_index_groups=cores)
+    rows = lax.all_gather(rows, "wide", axis=0, tiled=True, axis_index_groups=mixed)
+    other_rows = lax.ppermute(rows, "wide", [(i, i ^ 1) for i in range(wide)])
     terms = pl.pallas_call(
         functools.partial(pair_kernel, images),
         out_shape=jax.ShapeDtypeStruct((NEAR * images, width + LANES), jnp.bfloat16),
-        in_specs=[VMEM] * 3 + [SMEM] * 2,
+        in_specs=[VMEM] * 2 + [SMEM] * 2,
         out_specs=VMEM,
         compiler_params=pltpu.CompilerParams(vmem_limit_bytes=32 * 2**20),
         name="pair_terms",
-    )(pair_rows, other_rows, far_rows, logit_scale.reshape(1), logit_bias.reshape(1))
+    )(rows, other_rows, logit_scale.reshape(1), logit_bias.reshape(1))
     terms = lax.all_to_all(terms, "wide", 0, 0, tiled=True, axis_index_groups=near)
     row_loss, text_grad = pl.pallas_call(
         grad_kernel,

time: 65.4 us -> 60.9 us (0.931)
  starting transfers between devices: 6.14 us -> 3.12 us
  blocking collectives: 49.3 us -> 47.4 us
    ppermute x1, starting transfers between devices: 6.14 us -> 3.12 us  [shards(): other_rows = lax.ppermute(rows, 'wide', [(i, i ^ 1) for i in range(wide)])]
    all_gather x2, blocking collectives: 36.3 us -> 35.3 us  [the longest x1 19.4 us: shards(): lax.all_gather(rows, 'wide', axis=0, tiled=True, axis_index_groups=mixed)]
    all_to_all x1, blocking collectives: 13 us -> 12.1 us  [shards(): lax.all_to_all(terms, 'wide', 0, 0, tiled=True, axis_index_groups=near)]
  transfers between devices with their start and end apart: 1 -> 1, of which waited for: 0 -> 1; matrix products, arithmetic and copies ran while one was open for 0% -> 0% of each run, Pallas kernels for 0% -> 0%
where the time goes in v4:
time: 60.9 us; the launch traced here: 60.7 us
  blocking collectives  47.4 us (78%)
  Pallas kernels  7.79 us (13%)
  starting transfers between devices  3.12 us (5%)
  between operations  1.95 us (3%)
    all_gather x1, blocking collectives, shards(): lax.all_gather(rows, 'wide', axis=0, tiled=True, axis_index_groups=mixed)  19.4 us
    all_gather x1, blocking collectives, shards(): lax.all_gather(rows, 'wide', axis=0, tiled=True, axis_index_groups=cores)  15.9 us
    all_to_all x1, blocking collectives, shards(): lax.all_to_all(terms, 'wide', 0, 0, tiled=True, axis_index_groups=near)  12.1 us
    pallas_call x1, Pallas kernels, shards(): pl.pallas_call(pool_kernel, out_shape=jax.ShapeDtypeStruct((2 * images, w...  5.16 us
    ppermute x1, starting transfers between devices, shards(): other_rows = lax.ppermute(rows, 'wide', [(i, i ^ 1) for i in range(wide)])  3.12 us
    pallas_call x1, Pallas kernels, shards(): pl.pallas_call(grad_kernel, out_shape=(jax.ShapeDtypeStruct((1, images),...  1.75 us
  transfers between devices with their start and end apart: 1, of which 1 were waited for; matrix products, arithmetic and copies ran while one was open for 0% of the time, Pallas kernels for 0%

profile of v4, /device:TPU:1, one launch (start us, length us, event | category | flops | bytes accessed | tf_op | source)
XLA Modules:
  0.0 60.7 jit_solution(3880766879224265115)
XLA Ops:
  0.6 5.2 %pool_rows.1 = bf16[32,1280]{1,0:T(8,128)(2,1)} custom-call(bf16[16,16,1152]{2,1,0:T(8,128)(2,1)} %refs_0_.1, bf16[1152,1152]{1,0:T(8,128)(2,1)} %refs_1_.1, bf16[1152,1152]{1,0:T(8,128)(2,1)} %refs_2_.1, s32[16]{0:T(128)} %refs_3_.1, s32[16]{0:T(128)} %refs_4_.1, bf16[16,72]{1,0:T(8,128)(2,1)} %refs_5_.1, bf16[16,1152]{1,0:T(8,128)(2,1)} %text_ref.1), custom_call_target="tpu_custom_call" | custom-call | tf_op jit(solution)/shard_map/pool_rows/pallas_call | solution.py:191
  5.8 15.9 %all_gather.6 = bf16[64,1280]{1,0:T(8,128)(2,1)S(1)} all-gather(bf16[32,1280]{1,0:T(8,128)(2,1)} %pool_rows.1), channel_id=1, replica_groups={{0,32},{64,96},{128,160},{192,224},{256,288},{320,352},{384,416},{448,4..., dimensions={0}, use_global_device_ids=true | all-gather | bytes 245760 | tf_op jit(solution)/shard_map/all_gather | solution.py:201
  21.7 19.4 %all_gather.7.own_ref = bf16[256,1280]{1,0:T(8,128)(2,1)S(1)} all-gather(bf16[64,1280]{1,0:T(8,128)(2,1)S(1)} %all_gather.6), channel_id=1, replica_groups={{0,64,128,192},{256,320,384,448},{512,576,640,704},{768,832,896,960},{3..., dimensions={0}, use_global_device_ids=true | all-gather | bytes 819200 | tf_op jit(solution)/shard_map/all_gather | solution.py:202
  41.1 3.1 %collective-permute-start = (bf16[256,1280]{1,0:T(8,128)(2,1)S(1)}, bf16[256,1280]{1,0:T(8,128)(2,1)S(1)}, u32[]{:S(2)}, u32[]{:S(2)}) collective-permute-start(bf16[256,1280]{1,0:T(8,128)(2,1)S(1)} %all_gather.7.own_ref), channel_id=1, source_target_pairs={{0,32},{32,0},{64,96},{96,64},{128,160},{160,128},{192,224},{224,1... | collective-permute-start | bytes 1966088 | tf_op jit(solution)/shard_map/ppermute | solution.py:203
  45.5 0.4 collective-permute-done.other_ref
  45.9 0.9 %pair_terms.1 = bf16[64,1280]{1,0:T(8,128)(2,1)S(1)} custom-call(bf16[256,1280]{1,0:T(8,128)(2,1)S(1)} %all_gather.7.own_ref, bf16[256,1280]{1,0:T(8,128)(2,1)S(1)} %collective-permute-done.other_ref, f32[1]{0:T(128)} %bitcast.5.scale_ref, f32[1]{0:T(128)} %bitcast.6.bias_ref), custom_call_target="tpu_custom_call" | custom-call | tf_op jit(solution)/shard_map/pair_terms/pallas_call | solution.py:204
  46.8 12.1 %all_to_all.11 = bf16[4,16,1280]{2,1,0:T(8,128)(2,1)} all-to-all(bf16[4,16,1280]{2,1,0:T(8,128)(2,1)S(1)} %bitcast.7), channel_id=1, replica_groups={{0,64,128,192},{32,96,160,224},{256,320,384,448},{288,352,416,480},{512..., dimensions={0} | all-to-all | bytes 327680 | tf_op jit(solution)/shard_map/all_to_all | solution.py:212
  58.9 1.7 %text_gradient.1 = (f32[1,16]{1,0:T(1,128)}, f32[16,1152]{1,0:T(8,128)}) custom-call(bf16[64,1280]{1,0:T(8,128)(2,1)} %bitcast.8, bf16[16,1152]{1,0:T(8,128)(2,1)} %text_ref.1), custom_call_target="tpu_custom_call" | custom-call | tf_op jit(solution)/shard_map/text_gradient/pallas_call | solution.py:213
Async XLA Ops:
  41.1 4.8 %collective-permute-start = (bf16[256,1280]{1,0:T(8,128)(2,1)S(1)}, bf16[256,1280]{1,0:T(8,128)(2,1)S(1)}, u32[]{:S(2)}, u32[]{:S(2)}) collective-permute-start(bf16[256,1280]{1,0:T(8,128)(2,1)S(1)} %all_gather.7.own_ref), channel_id=1, source_target_pairs={{0,32},{32,0},{64,96},{96,64},{128,160},{160,128},{192,224},{224,1... | collective-permute-start | bytes 1966088 | tf_op jit(solution)/shard_map/ppermute | solution.py:203

commit v5 on v4

--- a/solution.py
+++ b/solution.py
@@ -38,6 +38,27 @@
 def wait(copies):
     for copy in copies:
         copy.wait()
+
+
+def put_rows(ref, first, rows):
+    images, width = rows.shape
+    for n in range(width // LANES):
+        at = 2 * images * n + first
+        ref[at : at + images] = rows[:, n * LANES : (n + 1) * LANES]
+
+
+def get_rows(ref, first, images, width):
+    step = 2 * images
+    return jnp.concatenate(
+        [ref[first + step * n : first + step * (n + 1)] for n in range(width // LANES)], axis=1
+    )
+
+
+def get_marks(ref, first, images, width, wide):
+    row, lane = iota((images, LANES), 0), iota((images, LANES), 1)
+    texts = jnp.where((lane == wide) | (lane == row + 32), 1.0, 0.0).astype(jnp.bfloat16)
+    first += 2 * images * width // LANES
+    return [texts, ref[first : first + images]]
 
 
 def pool_kernel(*refs):
@@ -61,12 +82,9 @@
     value_copy.start()
     text = text_ref[...].astype(jnp.float32)
     length = jnp.sqrt(jnp.sum(text * text, axis=-1, keepdims=True) + 1e-06)
-    out_ref[0:images, 0:width] = (text / length).astype(jnp.bfloat16)
-    wide = lax.axis_index("wide")
+    put_rows(out_ref, 0, (text / length).astype(jnp.bfloat16))
     lane = iota((images, LANES), 1)
     row = iota((images, LANES), 0)
-    place = (lane == wide) | (lane == row + 32)
-    out_ref[0:images, width:] = jnp.where(place, 1.0, 0.0).astype(jnp.bfloat16)
     first = jnp.zeros((images, LANES), jnp.int32)
     second = jnp.zeros((images, LANES), jnp.int32)
     valid = jnp.zeros((images, patch_count, heads), jnp.int32)
@@ -78,7 +96,7 @@
         second = jnp.where(row == i, label - 16 * high + 32, second)
         valid = jnp.where(image == i, counts_ref[i], valid)
     place = (lane == first) | (lane == second)
-    out_ref[images:, width:] = jnp.where(place, 1.0, 0.0).astype(jnp.bfloat16)
+    out_ref[2 * images * width // LANES :] = jnp.where(place, 1.0, 0.0).astype(jnp.bfloat16)
     valid = iota((images, patch_count, heads), 1) < valid
 
     column = iota((1, width), 1)
@@ -109,29 +127,43 @@
     pooled = jnp.sum(terms.reshape(images, patch_count, width), axis=1)
     pooled = pooled.astype(jnp.bfloat16).astype(jnp.float32)
     length = jnp.sqrt(jnp.sum(pooled * pooled, axis=-1, keepdims=True) + 1e-06)
-    out_ref[images:, 0:width] = (pooled / length).astype(jnp.bfloat16)
-
-
-def pair_kernel(images, own_ref, other_ref, scale_ref, bias_ref, out_ref):
-    core = lax.axis_index("wide") & 1
+    put_rows(out_ref, images, (pooled / length).astype(jnp.bfloat16))
+
+
+def pair_kernel(images, width, own_ref, other_ref, scale_ref, bias_ref, out_ref):
+    wide = lax.axis_index("wide")
+    core = wide & (CORES - 1)
     scale, bias = scale_ref[0], bias_ref[0]
     for this, (near_ref, far_ref) in enumerate(((own_ref, other_ref), (other_ref, own_ref))):
         pl.when(core == this)(
             functools.partial(
-                pair_terms, images, this, near_ref, far_ref, scale, bias, out_ref
+                pair_terms, images, width, wide, this, near_ref, far_ref, scale, bias, out_ref
             )
         )
 
 
-def pair_terms(images, core, near_ref, far_ref, scale, bias, out_ref):
-    rows = 2 * images
-    near_rows = jnp.concatenate(
-        [near_ref[pl.ds((CORES * n + core) * rows, rows)] for n in range(NEAR)]
-    )
-    near, width = near_rows.shape[0], near_rows.shape[1] - LANES
-    far = far_ref.shape[0]
-    raw = row_dot(near_rows[:, :width], far_ref[:, :width])
-    match = row_dot(near_rows[:, width:], far_ref[:, width:])
+def pair_terms(images, width, wide, core, near_ref, far_ref, scale, bias, out_ref):
+    size = 2 * images * width // LANES + images
+    block = CORES * NEAR
+    near_blocks = [
+        (near_ref, (CORES * n + core) * size, (wide & ~(block - 1)) + CORES * n + core)
+        for n in range(NEAR)
+    ]
+    far_blocks = [
+        (far_ref, n * size, (wide & (block - CORES)) + n // CORES * block + n % CORES)
+        for n in range(far_ref.shape[0] // size)
+    ]
+    near_rows, far_rows = (
+        jnp.concatenate([get_rows(ref, at, images, width) for ref, at, _ in blocks])
+        for blocks in (near_blocks, far_blocks)
+    )
+    near_marks, far_marks = (
+        jnp.concatenate(sum((get_marks(ref, at, images, width, w) for ref, at, w in blocks), []))
+        for blocks in (near_blocks, far_blocks)
+    )
+    near, far = near_rows.shape[0], far_rows.shape[0]
+    raw = row_dot(near_rows, far_rows)
+    match = row_dot(near_marks, far_marks)
     sign = jnp.where(match > 1.5, 1.0, -1.0)
     logits = -sign * (scale * raw + bias)
     small = jnp.exp(-jnp.abs(logits))
@@ -144,7 +176,7 @@
     loss = loss.reshape(NEAR, 2 * images, 1)[:, images:].reshape(NEAR * images, 1)
     high = slope.astype(jnp.bfloat16)
     low = (slope - high.astype(jnp.float32)).astype(jnp.bfloat16)
-    grad = scale * (dot(high, far_ref[:, :width]) + dot(low, far_ref[:, :width]))
+    grad = scale * (dot(high, far_rows) + dot(low, far_rows))
     lane = iota((NEAR * images, LANES), 1)
     parts = jnp.zeros((NEAR * images, LANES), jnp.float32)
     for n in range(3):
@@ -190,7 +222,9 @@
     places = (pltpu.VMEM,) * 3 + (pltpu.SMEM,) * 2 + (pltpu.VMEM,) * 2
     rows = pl.pallas_call(
         pool_kernel,
-        out_shape=jax.ShapeDtypeStruct((2 * images, width + LANES), jnp.bfloat16),
+        out_shape=jax.ShapeDtypeStruct(
+            (2 * images * width // LANES + images, LANES), jnp.bfloat16
+        ),
         in_specs=[ANY] * 7,
         out_specs=VMEM,
         scratch_shapes=[place(a.shape, a.dtype) for place, a in zip(places, arrays)]
@@ -202,7 +236,7 @@
     rows = lax.all_gather(rows, "wide", axis=0, tiled=True, axis_index_groups=mixed)
     other_rows = lax.ppermute(rows, "wide", [(i, i ^ 1) for i in range(wide)])
     terms = pl.pallas_call(
-        functools.partial(pair_kernel, images),
+        functools.partial(pair_kernel, images, width),
         out_shape=jax.ShapeDtypeStruct((NEAR * images, width + LANES), jnp.bfloat16),
         in_specs=[VMEM] * 2 + [SMEM] * 2,
         out_specs=VMEM,

time: 60.9 us -> 60.4 us (level)
  no operation moved by 1% of the time
where the time goes in v5:
time: 60.4 us; the launch traced here: 60.2 us
  blocking collectives  47.3 us (78%)
  Pallas kernels  7.8 us (13%)
  starting transfers between devices  2.79 us (5%)
  between operations  1.95 us (3%)
    all_gather x1, blocking collectives, shards(): lax.all_gather(rows, 'wide', axis=0, tiled=True, axis_index_groups=mixed)  19.3 us
    all_gather x1, blocking collectives, shards(): lax.all_gather(rows, 'wide', axis=0, tiled=True, axis_index_groups=cores)  15.9 us
    all_to_all x1, blocking collectives, shards(): lax.all_to_all(terms, 'wide', 0, 0, tiled=True, axis_index_groups=near)  12 us
    pallas_call x1, Pallas kernels, shards(): pl.pallas_call(pool_kernel, out_shape=jax.ShapeDtypeStruct((2 * images *...  5.16 us
    ppermute x1, starting transfers between devices, shards(): other_rows = lax.ppermute(rows, 'wide', [(i, i ^ 1) for i in range(wide)])  2.79 us
    pallas_call x1, Pallas kernels, shards(): pl.pallas_call(grad_kernel, out_shape=(jax.ShapeDtypeStruct((1, images),...  1.75 us
  transfers between devices with their start and end apart: 1, of which 1 were waited for; matrix products, arithmetic and copies ran while one was open for 0% of the time, Pallas kernels for 0%

profile of v5, /device:TPU:1, one launch (start us, length us, event | category | flops | bytes accessed | tf_op | source)
XLA Modules:
  0.0 60.2 jit_solution(12858609832789216033)
XLA Ops:
  0.6 5.2 %pool_rows.1 = bf16[304,128]{1,0:T(8,128)(2,1)} custom-call(bf16[16,16,1152]{2,1,0:T(8,128)(2,1)} %refs_0_.1, bf16[1152,1152]{1,0:T(8,128)(2,1)} %refs_1_.1, bf16[1152,1152]{1,0:T(8,128)(2,1)} %refs_2_.1, s32[16]{0:T(128)} %refs_3_.1, s32[16]{0:T(128)} %refs_4_.1, bf16[16,72]{1,0:T(8,128)(2,1)} %refs_5_.1, bf16[16,1152]{1,0:T(8,128)(2,1)} %text_ref.1), custom_call_target="tpu_custom_call" | custom-call | tf_op jit(solution)/shard_map/pool_rows/pallas_call | solution.py:223
  5.8 15.9 %all_gather.6 = bf16[608,128]{1,0:T(8,128)(2,1)S(1)} all-gather(bf16[304,128]{1,0:T(8,128)(2,1)} %pool_rows.1), channel_id=1, replica_groups={{0,32},{64,96},{128,160},{192,224},{256,288},{320,352},{384,416},{448,4..., dimensions={0}, use_global_device_ids=true | all-gather | bytes 233472 | tf_op jit(solution)/shard_map/all_gather | solution.py:235
  21.7 19.3 %all_gather.7.own_ref = bf16[2432,128]{1,0:T(8,128)(2,1)S(1)} all-gather(bf16[608,128]{1,0:T(8,128)(2,1)S(1)} %all_gather.6), channel_id=1, replica_groups={{0,64,128,192},{256,320,384,448},{512,576,640,704},{768,832,896,960},{3..., dimensions={0}, use_global_device_ids=true | all-gather | bytes 778240 | tf_op jit(solution)/shard_map/all_gather | solution.py:236
  41.0 2.8 %collective-permute-start = (bf16[2432,128]{1,0:T(8,128)(2,1)S(1)}, bf16[2432,128]{1,0:T(8,128)(2,1)S(1)}, u32[]{:S(2)}, u32[]{:S(2)}) collective-permute-start(bf16[2432,128]{1,0:T(8,128)(2,1)S(1)} %all_gather.7.own_ref), channel_id=1, source_target_pairs={{0,32},{32,0},{64,96},{96,64},{128,160},{160,128},{192,224},{224,1... | collective-permute-start | bytes 1867784 | tf_op jit(solution)/shard_map/ppermute | solution.py:237
  45.1 0.4 collective-permute-done.other_ref
  45.5 0.9 %pair_terms.1 = bf16[64,1280]{1,0:T(8,128)(2,1)S(1)} custom-call(bf16[2432,128]{1,0:T(8,128)(2,1)S(1)} %all_gather.7.own_ref, bf16[2432,128]{1,0:T(8,128)(2,1)S(1)} %collective-permute-done.other_ref, f32[1]{0:T(128)} %bitcast.5.scale_ref, f32[1]{0:T(128)} %bitcast.6.bias_ref), custom_call_target="tpu_custom_call" | custom-call | tf_op jit(solution)/shard_map/pair_terms/pallas_call | solution.py:238
  46.4 12.0 %all_to_all.11 = bf16[4,16,1280]{2,1,0:T(8,128)(2,1)} all-to-all(bf16[4,16,1280]{2,1,0:T(8,128)(2,1)S(1)} %bitcast.7), channel_id=1, replica_groups={{0,64,128,192},{32,96,160,224},{256,320,384,448},{288,352,416,480},{512..., dimensions={0} | all-to-all | bytes 327680 | tf_op jit(solution)/shard_map/all_to_all | solution.py:246
  58.4 1.7 %text_gradient.1 = (f32[1,16]{1,0:T(1,128)}, f32[16,1152]{1,0:T(8,128)}) custom-call(bf16[64,1280]{1,0:T(8,128)(2,1)} %bitcast.8, bf16[16,1152]{1,0:T(8,128)(2,1)} %text_ref.1), custom_call_target="tpu_custom_call" | custom-call | tf_op jit(solution)/shard_map/text_gradient/pallas_call | solution.py:247
Async XLA Ops:
  41.0 4.5 %collective-permute-start = (bf16[2432,128]{1,0:T(8,128)(2,1)S(1)}, bf16[2432,128]{1,0:T(8,128)(2,1)S(1)}, u32[]{:S(2)}, u32[]{:S(2)}) collective-permute-start(bf16[2432,128]{1,0:T(8,128)(2,1)S(1)} %all_gather.7.own_ref), channel_id=1, source_target_pairs={{0,32},{32,0},{64,96},{96,64},{128,160},{160,128},{192,224},{224,1... | collective-permute-start | bytes 1867784 | tf_op jit(solution)/shard_map/ppermute | solution.py:237

commit v6 on v5

--- a/solution.py
+++ b/solution.py
@@ -252,6 +252,7 @@
         ),
         in_specs=[VMEM, VMEM],
         out_specs=(VMEM, VMEM),
+        compiler_params=pltpu.CompilerParams(vmem_limit_bytes=32 * 2**20),
         name="text_gradient",
     )(terms, text_embed)
     return (row_loss.reshape(images), text_grad)

time: 60.4 us -> 59.4 us (0.983)
  Pallas kernels: 7.8 us -> 6.89 us
    pallas_call x1, Pallas kernels: 1.75 us -> 0.83 us  [shards(): pl.pallas_call(grad_kernel, out_shape=(jax.ShapeDtypeStruct((1, images),...]
where the time goes in v6:
time: 59.4 us; the launch traced here: 59.2 us
  blocking collectives  47.2 us (79%)
  Pallas kernels  6.89 us (12%)
  starting transfers between devices  2.79 us (5%)
  between operations  1.96 us (3%)
    all_gather x1, blocking collectives, shards(): lax.all_gather(rows, 'wide', axis=0, tiled=True, axis_index_groups=mixed)  19.3 us
    all_gather x1, blocking collectives, shards(): lax.all_gather(rows, 'wide', axis=0, tiled=True, axis_index_groups=cores)  15.9 us
    all_to_all x1, blocking collectives, shards(): lax.all_to_all(terms, 'wide', 0, 0, tiled=True, axis_index_groups=near)  11.9 us
    pallas_call x1, Pallas kernels, shards(): pl.pallas_call(pool_kernel, out_shape=jax.ShapeDtypeStruct((2 * images *...  5.16 us
    ppermute x1, starting transfers between devices, shards(): other_rows = lax.ppermute(rows, 'wide', [(i, i ^ 1) for i in range(wide)])  2.79 us
  transfers between devices with their start and end apart: 1, of which 1 were waited for; matrix products, arithmetic and copies ran while one was open for 0% of the time, Pallas kernels for 0%

profile of v6, /device:TPU:1, one launch (start us, length us, event | category | flops | bytes accessed | tf_op | source)
XLA Modules:
  0.0 59.2 jit_solution(5596098941799647067)
XLA Ops:
  0.6 5.2 %pool_rows.1 = bf16[304,128]{1,0:T(8,128)(2,1)} custom-call(bf16[16,16,1152]{2,1,0:T(8,128)(2,1)} %refs_0_.1, bf16[1152,1152]{1,0:T(8,128)(2,1)} %refs_1_.1, bf16[1152,1152]{1,0:T(8,128)(2,1)} %refs_2_.1, s32[16]{0:T(128)} %refs_3_.1, s32[16]{0:T(128)} %refs_4_.1, bf16[16,72]{1,0:T(8,128)(2,1)} %refs_5_.1, bf16[16,1152]{1,0:T(8,128)(2,1)} %text_ref.1), custom_call_target="tpu_custom_call" | custom-call | tf_op jit(solution)/shard_map/pool_rows/pallas_call | solution.py:223
  5.8 0.0 copy-start
  5.8 15.9 %all_gather.6 = bf16[608,128]{1,0:T(8,128)(2,1)S(1)} all-gather(bf16[304,128]{1,0:T(8,128)(2,1)} %pool_rows.1), channel_id=1, replica_groups={{0,32},{64,96},{128,160},{192,224},{256,288},{320,352},{384,416},{448,4..., dimensions={0}, use_global_device_ids=true | all-gather | bytes 233472 | tf_op jit(solution)/shard_map/all_gather | solution.py:235
  21.7 19.3 %all_gather.7.own_ref = bf16[2432,128]{1,0:T(8,128)(2,1)S(1)} all-gather(bf16[608,128]{1,0:T(8,128)(2,1)S(1)} %all_gather.6), channel_id=1, replica_groups={{0,64,128,192},{256,320,384,448},{512,576,640,704},{768,832,896,960},{3..., dimensions={0}, use_global_device_ids=true | all-gather | bytes 778240 | tf_op jit(solution)/shard_map/all_gather | solution.py:236
  41.1 2.8 %collective-permute-start = (bf16[2432,128]{1,0:T(8,128)(2,1)S(1)}, bf16[2432,128]{1,0:T(8,128)(2,1)S(1)}, u32[]{:S(2)}, u32[]{:S(2)}) collective-permute-start(bf16[2432,128]{1,0:T(8,128)(2,1)S(1)} %all_gather.7.own_ref), channel_id=1, source_target_pairs={{0,32},{32,0},{64,96},{96,64},{128,160},{160,128},{192,224},{224,1... | collective-permute-start | bytes 1867784 | tf_op jit(solution)/shard_map/ppermute | solution.py:237
  45.1 0.4 collective-permute-done.other_ref
  45.5 0.9 %pair_terms.1 = bf16[64,1280]{1,0:T(8,128)(2,1)S(1)} custom-call(bf16[2432,128]{1,0:T(8,128)(2,1)S(1)} %all_gather.7.own_ref, bf16[2432,128]{1,0:T(8,128)(2,1)S(1)} %collective-permute-done.other_ref, f32[1]{0:T(128)} %bitcast.5.scale_ref, f32[1]{0:T(128)} %bitcast.6.bias_ref), custom_call_target="tpu_custom_call" | custom-call | tf_op jit(solution)/shard_map/pair_terms/pallas_call | solution.py:238
  46.4 11.9 %all_to_all.11 = bf16[4,16,1280]{2,1,0:T(8,128)(2,1)S(1)} all-to-all(bf16[4,16,1280]{2,1,0:T(8,128)(2,1)S(1)} %bitcast.7), channel_id=1, replica_groups={{0,64,128,192},{32,96,160,224},{256,320,384,448},{288,352,416,480},{512..., dimensions={0} | all-to-all | bytes 327680 | tf_op jit(solution)/shard_map/all_to_all | solution.py:246
  58.3 0.0 copy-done
  58.3 0.8 %text_gradient.1 = (f32[1,16]{1,0:T(1,128)}, f32[16,1152]{1,0:T(8,128)}) custom-call(bf16[64,1280]{1,0:T(8,128)(2,1)S(1)} %bitcast.8, bf16[16,1152]{1,0:T(8,128)(2,1)S(1)} %copy-done), custom_call_target="tpu_custom_call" | custom-call | tf_op jit(solution)/shard_map/text_gradient/pallas_call | solution.py:247
Async XLA Ops:
  5.8 52.5 %copy-start = (bf16[16,1152]{1,0:T(8,128)(2,1)S(1)}, bf16[16,1152]{1,0:T(8,128)(2,1)}, u32[]{:S(2)}) copy-start(bf16[16,1152]{1,0:T(8,128)(2,1)} %text_ref.1) | copy-start | bytes 110596
  41.1 4.5 %collective-permute-start = (bf16[2432,128]{1,0:T(8,128)(2,1)S(1)}, bf16[2432,128]{1,0:T(8,128)(2,1)S(1)}, u32[]{:S(2)}, u32[]{:S(2)}) collective-permute-start(bf16[2432,128]{1,0:T(8,128)(2,1)S(1)} %all_gather.7.own_ref), channel_id=1, source_target_pairs={{0,32},{32,0},{64,96},{96,64},{128,160},{160,128},{192,224},{224,1... | collective-permute-start | bytes 1867784 | tf_op jit(solution)/shard_map/ppermute | solution.py:237

commit v7 on v6

--- a/solution.py
+++ b/solution.py
@@ -117,13 +117,13 @@
         keys = dot(flat, key_ref[:, at]).astype(jnp.bfloat16)
         scores += row_dot(keys, query[:, at])
     value_copy.wait()
-    values = dot(flat, value_ref[...]).astype(jnp.bfloat16)
+    values = dot(flat, value_ref[...])
     scores = (scores * (1.0 / head_size**0.5)).reshape(images, patch_count, heads)
     scores = jnp.where(valid, scores, -1e30)
     scores = jnp.exp(scores - jnp.max(scores, axis=1, keepdims=True))
     attend = scores / jnp.sum(scores, axis=1, keepdims=True)
     attend = attend.reshape(rows, heads).astype(jnp.bfloat16)
-    terms = dot(attend, own) * values.astype(jnp.float32)
+    terms = dot(attend, own) * values
     pooled = jnp.sum(terms.reshape(images, patch_count, width), axis=1)
     pooled = pooled.astype(jnp.bfloat16).astype(jnp.float32)
     length = jnp.sqrt(jnp.sum(pooled * pooled, axis=-1, keepdims=True) + 1e-06)

time: 59.4 us -> 59.4 us (level)
  no operation moved by 1% of the time
where the time goes in v7:
time: 59.4 us; the launch traced here: 59.2 us
  blocking collectives  47.2 us (79%)
  Pallas kernels  6.88 us (12%)
  starting transfers between devices  2.79 us (5%)
  between operations  1.96 us (3%)
    all_gather x1, blocking collectives, shards(): lax.all_gather(rows, 'wide', axis=0, tiled=True, axis_index_groups=mixed)  19.3 us
    all_gather x1, blocking collectives, shards(): lax.all_gather(rows, 'wide', axis=0, tiled=True, axis_index_groups=cores)  15.9 us
    all_to_all x1, blocking collectives, shards(): lax.all_to_all(terms, 'wide', 0, 0, tiled=True, axis_index_groups=near)  11.9 us
    pallas_call x1, Pallas kernels, shards(): pl.pallas_call(pool_kernel, out_shape=jax.ShapeDtypeStruct((2 * images *...  5.15 us
    ppermute x1, starting transfers between devices, shards(): other_rows = lax.ppermute(rows, 'wide', [(i, i ^ 1) for i in range(wide)])  2.79 us
  transfers between devices with their start and end apart: 1, of which 1 were waited for; matrix products, arithmetic and copies ran while one was open for 0% of the time, Pallas kernels for 0%

profile of v7, /device:TPU:1, one launch (start us, length us, event | category | flops | bytes accessed | tf_op | source)
XLA Modules:
  0.0 59.2 jit_solution(5064251319334070645)
XLA Ops:
  0.6 5.1 %pool_rows.1 = bf16[304,128]{1,0:T(8,128)(2,1)} custom-call(bf16[16,16,1152]{2,1,0:T(8,128)(2,1)} %refs_0_.1, bf16[1152,1152]{1,0:T(8,128)(2,1)} %refs_1_.1, bf16[1152,1152]{1,0:T(8,128)(2,1)} %refs_2_.1, s32[16]{0:T(128)} %refs_3_.1, s32[16]{0:T(128)} %refs_4_.1, bf16[16,72]{1,0:T(8,128)(2,1)} %refs_5_.1, bf16[16,1152]{1,0:T(8,128)(2,1)} %text_ref.1), custom_call_target="tpu_custom_call" | custom-call | tf_op jit(solution)/shard_map/pool_rows/pallas_call | solution.py:223
  5.8 0.0 copy-start
  5.8 15.9 %all_gather.6 = bf16[608,128]{1,0:T(8,128)(2,1)S(1)} all-gather(bf16[304,128]{1,0:T(8,128)(2,1)} %pool_rows.1), channel_id=1, replica_groups={{0,32},{64,96},{128,160},{192,224},{256,288},{320,352},{384,416},{448,4..., dimensions={0}, use_global_device_ids=true | all-gather | bytes 233472 | tf_op jit(solution)/shard_map/all_gather | solution.py:235
  21.7 19.3 %all_gather.7.own_ref = bf16[2432,128]{1,0:T(8,128)(2,1)S(1)} all-gather(bf16[608,128]{1,0:T(8,128)(2,1)S(1)} %all_gather.6), channel_id=1, replica_groups={{0,64,128,192},{256,320,384,448},{512,576,640,704},{768,832,896,960},{3..., dimensions={0}, use_global_device_ids=true | all-gather | bytes 778240 | tf_op jit(solution)/shard_map/all_gather | solution.py:236
  41.0 2.8 %collective-permute-start = (bf16[2432,128]{1,0:T(8,128)(2,1)S(1)}, bf16[2432,128]{1,0:T(8,128)(2,1)S(1)}, u32[]{:S(2)}, u32[]{:S(2)}) collective-permute-start(bf16[2432,128]{1,0:T(8,128)(2,1)S(1)} %all_gather.7.own_ref), channel_id=1, source_target_pairs={{0,32},{32,0},{64,96},{96,64},{128,160},{160,128},{192,224},{224,1... | collective-permute-start | bytes 1867784 | tf_op jit(solution)/shard_map/ppermute | solution.py:237
  45.1 0.4 collective-permute-done.other_ref
  45.5 0.9 %pair_terms.1 = bf16[64,1280]{1,0:T(8,128)(2,1)S(1)} custom-call(bf16[2432,128]{1,0:T(8,128)(2,1)S(1)} %all_gather.7.own_ref, bf16[2432,128]{1,0:T(8,128)(2,1)S(1)} %collective-permute-done.other_ref, f32[1]{0:T(128)} %bitcast.5.scale_ref, f32[1]{0:T(128)} %bitcast.6.bias_ref), custom_call_target="tpu_custom_call" | custom-call | tf_op jit(solution)/shard_map/pair_terms/pallas_call | solution.py:238
  46.4 11.9 %all_to_all.11 = bf16[4,16,1280]{2,1,0:T(8,128)(2,1)S(1)} all-to-all(bf16[4,16,1280]{2,1,0:T(8,128)(2,1)S(1)} %bitcast.7), channel_id=1, replica_groups={{0,64,128,192},{32,96,160,224},{256,320,384,448},{288,352,416,480},{512..., dimensions={0} | all-to-all | bytes 327680 | tf_op jit(solution)/shard_map/all_to_all | solution.py:246
  58.3 0.0 copy-done
  58.3 0.8 %text_gradient.1 = (f32[1,16]{1,0:T(1,128)}, f32[16,1152]{1,0:T(8,128)}) custom-call(bf16[64,1280]{1,0:T(8,128)(2,1)S(1)} %bitcast.8, bf16[16,1152]{1,0:T(8,128)(2,1)S(1)} %copy-done), custom_call_target="tpu_custom_call" | custom-call | tf_op jit(solution)/shard_map/text_gradient/pallas_call | solution.py:247
Async XLA Ops:
  5.8 52.5 %copy-start = (bf16[16,1152]{1,0:T(8,128)(2,1)S(1)}, bf16[16,1152]{1,0:T(8,128)(2,1)}, u32[]{:S(2)}) copy-start(bf16[16,1152]{1,0:T(8,128)(2,1)} %text_ref.1) | copy-start | bytes 110596
  41.0 4.5 %collective-permute-start = (bf16[2432,128]{1,0:T(8,128)(2,1)S(1)}, bf16[2432,128]{1,0:T(8,128)(2,1)S(1)}, u32[]{:S(2)}, u32[]{:S(2)}) collective-permute-start(bf16[2432,128]{1,0:T(8,128)(2,1)S(1)} %all_gather.7.own_ref), channel_id=1, source_target_pairs={{0,32},{32,0},{64,96},{96,64},{128,160},{160,128},{192,224},{224,1... | collective-permute-start | bytes 1867784 | tf_op jit(solution)/shard_map/ppermute | solution.py:237
